TPU v7x, 256 devices: a whole 4x4x8 slice. The times are simulated.
256 devices in a mesh: dp: 64 (over y_lo, x, z), mp: 4 (over y_hi, core).
Axes of the slice: x: 4, y: 4 (y_hi: 2, y_lo: 2; y = y_hi * 2 + y_lo), z: 8, core: 2. Of those that a mesh axis runs over, the one named last changes fastest.
Arguments:
- img_feats: bfloat16 [131072, 1024], P('dp'), may hold values from -64 to 64
- txt_feats: bfloat16 [131072, 768], P('dp'), may hold values from -64 to 64
- img_weight: bfloat16 [1024, 768], P(None, 'mp'), may hold values from -1 to 1
- txt_weight: bfloat16 [768, 768], P(None, 'mp'), may hold values from -1 to 1
- row_lse: float32 [131072], P(('dp', 'mp')), may hold values from 10 to 16
- col_lse: float32 [131072], P('dp'), may hold values from 10 to 16
- labels: int32 [64, 2048], P('dp'), may hold values from 0 to 2047, as said below
Outputs:
- img_weight_grad: float32 [1024, 768], P(None, 'mp')
- txt_grad: float32 [131072, 768], P('dp', 'mp')
Inputs may be any that keep to these rules, and one draw needn't show every extreme that they name: Each row of labels is a permutation of 0 to 2047.
All inputs are finite; a program needn't handle non-finite values.
Results may differ from a plain program's by a relative error of at most 0.004.
Values may be sent and summed in bfloat16 or wider, within the bound.
No kernel may reach another device: no remote copies, remote signals or barrier semaphores. Data moves between devices by JAX's collectives and lax.ppermute only.
A program may use at most 128 MiB of HBM per device.

v0:
```python
import functools
import math

import jax
import jax.numpy as jnp
from jax import lax
from jax.experimental import pallas as pl
from jax.experimental.pallas import tpu as pltpu
from jax.sharding import Mesh, PartitionSpec as P

scale_logit = 1.0 / 0.07
loss_weight = 0.25
epsilon = 1e-06
exp_scale = scale_logit * math.log2(math.e)

AXES = ("yl", "x", "z", "yh", "core")
DP = ("yl", "x", "z")
MP = ("yh", "core")
BF = jnp.bfloat16
F32 = jnp.float32
VMEM_LIMIT = 56 * 1024 * 1024
TXT_CHUNK, IMG_CHUNK = 512, 1024

NT = (((1,), (1,)), ((), ()))
NN = (((1,), (0,)), ((), ()))


def dot(a, b, dims):
    return lax.dot_general(a, b, dims, preferred_element_type=F32)


def routes(sizes, move):
    n_yl, n_x, n_z, n_yh, n_core = sizes

    def flat(p):
        yl, x, z, yh, core = p
        return (((yl * n_x + x) * n_z + z) * n_yh + yh) * n_core + core

    pairs = []
    for yl in range(n_yl):
        for x in range(n_x):
            for z in range(n_z):
                for yh in range(n_yh):
                    for core in range(n_core):
                        p = (yl, x, z, yh, core)
                        pairs.append((flat(p), flat(move(*p))))
    return pairs


VMEM = pl.BlockSpec(memory_space=pltpu.VMEM)
ANY = pl.BlockSpec(memory_space=pl.ANY)


def call(body, ins, outs, scratch, flops, bytes_accessed, transcendentals=0):
    return pl.pallas_call(
        body,
        out_shape=[shape for shape, _ in outs],
        in_specs=ins,
        out_specs=[spec for _, spec in outs],
        scratch_shapes=scratch,
        compiler_params=pltpu.CompilerParams(vmem_limit_bytes=VMEM_LIMIT),
        cost_estimate=pl.CostEstimate(
            flops=0, bytes_accessed=0, transcendentals=0
        ),
    )


def copies(pairs, sems):
    made = [pltpu.make_async_copy(a, b, sems.at[n]) for n, (a, b) in enumerate(pairs)]
    for c in made:
        c.start()
    return made


def near_kernel(
    img_hbm, txt_hbm, w0, w1, row_ref,
    img_raw, txt_raw, er_ref,
    img_s, txt_s, wi_s, wt_s, sems,
):
    txt_in, img_in = copies([(txt_hbm, txt_s), (img_hbm, img_s)], sems)
    er_ref[...] = loss_weight * jnp.exp(-row_ref[...])
    cols = w0.shape[0]
    depth = wi_s.shape[1]
    for n, w in enumerate((w0, w1)):
        wi_s[n * cols : (n + 1) * cols, :] = w[:, 0:depth]
        wt_s[n * cols : (n + 1) * cols, :] = w[:, depth:]
    pairs = img_s.shape[0]
    txt_in.wait()
    for r in range(0, pairs, 512):
        txt_raw[r : r + 512, :] = dot(txt_s[r : r + 512, :], wt_s[...], NT)
    img_in.wait()
    for r in range(0, pairs, 512):
        img_raw[:, r : r + 512] = dot(wi_s[...], img_s[r : r + 512, :], NT)


def stand(lse_ref, first, column_ref):
    for n in range(column_ref.shape[0] // 128):
        weight = loss_weight * jnp.exp(-lse_ref[pl.ds(first + n, 1), :])
        column_ref[n * 128 : (n + 1) * 128, :] = jnp.transpose(jnp.broadcast_to(weight, (128, 128)))


def score_tile(
    txt_emb, txt_own_t, img_emb_t, er_ref, ec_s, label_ref, g_s, finish, txt_chunk, img_chunk
):
    texts = txt_emb.shape[0]
    images = img_emb_t.shape[1]
    cols = txt_own_t.shape[0]
    for i in range(0, images, img_chunk):
        at = slice(i, i + img_chunk)
        img_part = jnp.zeros((cols, img_chunk), F32)
        along = jnp.zeros((1, img_chunk), F32)
        er = er_ref[:, at]
        for t in range(0, texts, txt_chunk):
            raw = dot(txt_emb[t : t + txt_chunk, :], img_emb_t[:, at], NN)
            g = jnp.exp2(raw * exp_scale) * (er + ec_s[t : t + txt_chunk, 0:1])
            if label_ref is not None:
                place = lax.broadcasted_iota(jnp.int32, (txt_chunk, img_chunk), 0)
                g = g - jnp.where(place == (label_ref[:, at] - t), 2.0 * loss_weight, 0.0)
            g = g.astype(BF)
            along = along + jnp.sum(g.astype(F32) * raw, 0, keepdims=True)
            img_part = img_part + dot(txt_own_t[:, t : t + txt_chunk], g, NN)
            g_s[t : t + txt_chunk, at] = g
        finish(at, img_part, along)


def text_part(g_s, img_emb_t, cols, out_ref):
    for t in range(0, g_s.shape[0], 256):
        out_ref[:, t : t + 256] = (
            scale_logit * dot(img_emb_t[0:cols, :], g_s[t : t + 256, :], NT)
        ).astype(out_ref.dtype)


def first_kernel(
    txt_hbm, txt_raw_hbm, img_hbm, img_raw_hbm, w0, w1, w2, w3, er_ref, col_ref, label_ref,
    img_emb_hbm, img_own_hbm, wt_hbm, inv_ref, img_part_ref, along_ref, txt_part_ref,
    txt_s, txt_raw, img_s, img_raw, wi_s, wt_s, txt_emb, txt_own_t, img_emb_t, img_own_t, ec_s, g_s,
    sems, out_sems,
):
    loads = copies(
        [(txt_hbm, txt_s), (txt_raw_hbm, txt_raw), (img_hbm, img_s), (img_raw_hbm, img_raw)], sems
    )
    cols = w0.shape[0]
    depth = wi_s.shape[1]
    for n, w in enumerate((w0, w1, w2, w3)):
        wt_s[n * cols : (n + 1) * cols, :] = w[:, depth:]
    for n, w in enumerate((w2, w3)):
        wi_s[n * cols : (n + 1) * cols, :] = w[:, 0:depth]
    stand(col_ref, 0, ec_s)
    save_wt = pltpu.make_async_copy(wt_s, wt_hbm, out_sems.at[0])
    save_wt.start()
    pairs = txt_s.shape[0]
    two = 2 * cols
    loads[0].wait()
    loads[1].wait()
    for r in range(0, pairs, 512):
        far = dot(txt_s[r : r + 512, :], wt_s[two:, :], NT)
        near = txt_raw[r : r + 512, :]
        total = jnp.sum(near * near, -1, keepdims=True) + jnp.sum(far * far, -1, keepdims=True)
        inv = lax.rsqrt(total + epsilon)
        near = near * inv
        txt_emb[r : r + 512, 0:two] = near.astype(BF)
        txt_emb[r : r + 512, two:] = (far * inv).astype(BF)
        txt_own_t[:, r : r + 512] = jnp.transpose(near[:, 0:256])[0:cols, :].astype(BF)
    loads[2].wait()
    loads[3].wait()
    for r in range(0, pairs, 512):
        at = slice(r, r + 512)
        far = dot(wi_s[...], img_s[at, :], NT)
        near = img_raw[:, at]
        total = jnp.sum(near * near, 0, keepdims=True) + jnp.sum(far * far, 0, keepdims=True)
        inv = lax.rsqrt(total + epsilon)
        near = near * inv
        img_emb_t[0:two, at] = near.astype(BF)
        img_emb_t[two:, at] = (far * inv).astype(BF)
        img_own_t[:, at] = near[0:cols, :]
        inv_ref[:, at] = inv
    saves = [
        pltpu.make_async_copy(img_emb_t, img_emb_hbm, out_sems.at[1]),
        pltpu.make_async_copy(img_own_t, img_own_hbm, out_sems.at[2]),
    ]
    for c in saves:
        c.start()

    def finish(at, img_part, along):
        img_part_ref[:, at] = img_part
        along_ref[:, at] = along

    score_tile(
        txt_emb, txt_own_t, img_emb_t, er_ref, ec_s, label_ref, g_s, finish, TXT_CHUNK, IMG_CHUNK
    )
    text_part(g_s, img_emb_t, cols, txt_part_ref)
    save_wt.wait()
    for c in saves:
        c.wait()


def project_texts(feats_ref, wt_ref, emb_ref, own_t_ref):
    cols = own_t_ref.shape[0]
    for r in range(0, emb_ref.shape[0], 512):
        raw = dot(feats_ref[r : r + 512, :], wt_ref[...], NT)
        unit = raw * lax.rsqrt(jnp.sum(raw * raw, -1, keepdims=True) + epsilon)
        emb_ref[r : r + 512, :] = unit.astype(BF)
        own_t_ref[:, r : r + 512] = jnp.transpose(unit[:, 0:256])[0:cols, :].astype(BF)


def stand_half(feats, place, lse_s, ec_s):
    half = ec_s.shape[0]
    parts = [feats[half:, n * 128 : (n + 1) * 128].astype(F32) for n in range(3)]
    lse_s[...] = (parts[0] + parts[1]) + parts[2]
    stand(lse_s, place * (half // 128), ec_s)


def second_kernel(
    feats, wt, img_emb_hbm, er_ref, img_part_hbm, along_in,
    img_part_ref, along_ref, txt_part_ref,
    img_emb_t, img_part_s, txt_emb, txt_own_t, lse_s, ec_s, g_s, sems,
):
    loads = copies([(img_emb_hbm, img_emb_t), (img_part_hbm, img_part_s)], sems)
    stand_half(feats, lax.axis_index("core"), lse_s, ec_s)
    project_texts(feats, wt, txt_emb, txt_own_t)
    for c in loads:
        c.wait()

    def finish(at, img_part, along):
        img_part_ref[:, at] = img_part_s[:, at] + img_part
        along_ref[:, at] = along_in[:, at] + along

    score_tile(
        txt_emb, txt_own_t, img_emb_t, er_ref, ec_s, None, g_s, finish, TXT_CHUNK, IMG_CHUNK
    )
    text_part(g_s, img_emb_t, txt_own_t.shape[0], txt_part_ref)


def last_kernel(
    feats, wt, img_emb_hbm, er_ref, img_part_hbm, along_in, img_own_hbm, inv_ref, img_hbm,
    pieces_ref, txt_part_ref,
    img_emb_t, img_part_s, img_own_t, img_s, txt_emb, txt_own_t, lse_s, ec_s, g_s, d_raw, sems,
):
    loads = copies(
        [
            (img_emb_hbm, img_emb_t), (img_part_hbm, img_part_s),
            (img_own_hbm, img_own_t), (img_hbm, img_s),
        ],
        sems,
    )
    stand_half(feats, 1 - lax.axis_index("core"), lse_s, ec_s)
    project_texts(feats, wt, txt_emb, txt_own_t)
    for c in loads:
        c.wait()

    def finish(at, img_part, along):
        grad = img_part_s[:, at] + img_part
        toward = along_in[:, at] + along
        d_raw[:, at] = (
            (grad - img_own_t[:, at] * toward) * (scale_logit * inv_ref[:, at])
        ).astype(BF)

    score_tile(
        txt_emb, txt_own_t, img_emb_t, er_ref, ec_s, None, g_s, finish, TXT_CHUNK, IMG_CHUNK
    )
    n_pieces, rb, cb = pieces_ref.shape
    across = img_s.shape[1] // cb
    for k in range(0, img_s.shape[1], 256):
        part = dot(d_raw[...], img_s[:, k : k + 256], NN)
        for r in range(n_pieces // across):
            for c in range(256 // cb):
                pieces_ref[r * across + k // cb + c] = part[
                    r * rb : (r + 1) * rb, c * cb : (c + 1) * cb
                ].astype(BF)
    text_part(g_s, img_emb_t, txt_own_t.shape[0], txt_part_ref)


def text_total_kernel(part_a, part_b, carry, out_ref):
    half = part_a.shape[1]
    core = lax.axis_index("core")
    for place, part in ((core, part_a), (1 - core, part_b)):
        at = pl.ds(pl.multiple_of(place * half, half), half)
        out_ref[:, at] = part[...] + carry[:, at].astype(F32)


def local(sizes, img_feats, txt_feats, img_weight, txt_weight, row_lse, col_lse, labels):
    n_yl, n_x, n_z, n_yh, n_core = sizes
    n_dp = n_yl * n_x * n_z
    pairs = img_feats.shape[0]
    cols = img_weight.shape[1]
    width = cols * n_yh * n_core
    img_in, txt_in = img_feats.shape[1], txt_feats.shape[1]
    core = lax.axis_index("core")
    yh = lax.axis_index("yh")

    across = routes(sizes, lambda yl, x, z, h, c: (1 - yl, x, z, 1 - h, c))
    swap = routes(sizes, lambda yl, x, z, h, c: (yl, x, z, h, 1 - c))
    peer = routes(sizes, lambda yl, x, z, h, c: (yl, x, z, 1 - h, c))

    cross = routes(sizes, lambda yl, x, z, h, c: (yl, x, z, 1 - h, 1 - c))

    def following(yl, x, z, h, c):
        d = ((yl * n_x + x) * n_z + z + 1) % n_dp
        return (d // (n_x * n_z), (d // n_z) % n_x, d % n_z, h, c)

    onward = routes(sizes, following)

    def send(a, route):
        return lax.ppermute(a, AXES, route)

    def ordered(bit, own, other):
        first = jnp.where(bit == 0, own, other)
        second = jnp.where(bit == 0, other, own)
        return jnp.concatenate([first, second], 1)

    shape = jax.ShapeDtypeStruct
    half = pairs // n_core
    w_own = jnp.concatenate([img_weight.T, txt_weight.T], 1)
    w_far = send(w_own, across)
    w_near = send(w_own, swap)
    w_far_near = send(w_far, swap)
    lse = col_lse.reshape(pairs // 128, 128)
    high = lax.reduce_precision(lse, 8, 7)
    middle = lax.reduce_precision(lse - high, 8, 7)
    low = (lse - high) - middle
    lse_rows = jnp.concatenate([high, middle, low], 1).astype(BF)
    lse_rows = jnp.pad(lse_rows, ((0, 0), (0, txt_in - 3 * 128)))
    mine = lax.dynamic_slice_in_dim(txt_feats, core * half, half, 0)
    feats_a = send(jnp.concatenate([mine, lse_rows], 0), onward)

    img_raw, txt_raw, er_own = call(
        near_kernel,
        [ANY, ANY, VMEM, VMEM, VMEM],
        [
            (shape((2 * cols, pairs), F32), VMEM),
            (shape((pairs, 2 * cols), F32), VMEM),
            (shape((1, row_lse.shape[0]), F32), VMEM),
        ],
        [
            pltpu.VMEM((pairs, img_in), BF),
            pltpu.VMEM((pairs, txt_in), BF),
            pltpu.VMEM((2 * cols, img_in), BF),
            pltpu.VMEM((2 * cols, txt_in), BF),
            pltpu.SemaphoreType.DMA((2,)),
        ],
        2 * pairs * 2 * cols * (img_in + txt_in),
        2 * pairs * (img_in + txt_in + 2 * width),
    )(img_feats, txt_feats, w_own, w_near, row_lse[None, :])
    er_near = send(er_own, swap)
    er_far = send(er_own, peer)
    er_far_near = send(er_own, cross)
    er = ordered(yh, ordered(core, er_own, er_near), ordered(core, er_far, er_far_near))

    tile_flops = 2 * pairs * pairs * (width + 2 * cols)
    img_emb_t, img_own_t, wt, inv, img_part, along, txt_part = call(
        first_kernel,
        [ANY] * 4 + [VMEM] * 7,
        [
            (shape((width, pairs), BF), ANY),
            (shape((cols, pairs), F32), ANY),
            (shape((width, txt_in), BF), ANY),
            (shape((1, pairs), F32), VMEM),
            (shape((cols, pairs), F32), VMEM),
            (shape((1, pairs), F32), VMEM),
            (shape((cols, pairs), BF), VMEM),
        ],
        [
            pltpu.VMEM((pairs, txt_in), BF),
            pltpu.VMEM((pairs, 2 * cols), F32),
            pltpu.VMEM((pairs, img_in), BF),
            pltpu.VMEM((2 * cols, pairs), F32),
            pltpu.VMEM((2 * cols, img_in), BF),
            pltpu.VMEM((width, txt_in), BF),
            pltpu.VMEM((pairs, width), BF),
            pltpu.VMEM((cols, pairs), BF),
            pltpu.VMEM((width, pairs), BF),
            pltpu.VMEM((cols, pairs), F32),
            pltpu.VMEM((pairs, 128), F32),
            pltpu.VMEM((pairs, pairs), BF),
            pltpu.SemaphoreType.DMA((4,)),
            pltpu.SemaphoreType.DMA((3,)),
        ],
        tile_flops,
        4 * pairs * width * 2,
        pairs * pairs,
    )(
        txt_feats, txt_raw, img_feats, img_raw, w_own, w_near, w_far, w_far_near, er, lse, labels
    )
    txt_carry = send(txt_part, onward)
    feats_a, along = lax.optimization_barrier((feats_a, along))
    feats_b = send(feats_a, swap)

    half_scratch = [
        pltpu.VMEM((half, width), BF),
        pltpu.VMEM((cols, half), BF),
        pltpu.VMEM((pairs // 128, 128), F32),
        pltpu.VMEM((half, 128), F32),
        pltpu.VMEM((half, pairs), BF),
    ]
    img_part, along, txt_a = call(
        second_kernel,
        [VMEM, VMEM, ANY, VMEM, ANY, VMEM],
        [
            (shape((cols, pairs), F32), VMEM),
            (shape((1, pairs), F32), VMEM),
            (shape((cols, half), F32), VMEM),
        ],
        [pltpu.VMEM((width, pairs), BF), pltpu.VMEM((cols, pairs), F32)]
        + half_scratch
        + [pltpu.SemaphoreType.DMA((2,))],
        tile_flops // 2,
        2 * pairs * width * 2,
        pairs * half,
    )(feats_a, wt, img_emb_t, er, img_part, along)
    pieces, txt_b = call(
        last_kernel,
        [VMEM, VMEM, ANY, VMEM, ANY, VMEM, ANY, VMEM, ANY],
        [(shape((n_dp, cols * img_in // (128 * n_dp), 128), BF), VMEM), (shape((cols, half), F32), VMEM)],
        [
            pltpu.VMEM((width, pairs), BF),
            pltpu.VMEM((cols, pairs), F32),
            pltpu.VMEM((cols, pairs), F32),
            pltpu.VMEM((pairs, img_in), BF),
        ]
        + half_scratch
        + [pltpu.VMEM((cols, pairs), BF), pltpu.SemaphoreType.DMA((4,))],
        tile_flops // 2,
        2 * pairs * width * 2,
        pairs * half,
    )(feats_b, wt, img_emb_t, er, img_part, along, img_own_t, inv, img_feats)

    pieces, txt_carry = lax.optimization_barrier((pieces, txt_carry))
    got = lax.all_to_all(pieces, DP, 0, 0, tiled=True)
    total = jnp.sum(got.astype(F32), 0).astype(BF)
    spread = jnp.broadcast_to(total[None], pieces.shape)
    back = lax.all_to_all(spread, DP, 0, 0, tiled=True)
    (txt_total,) = call(
        text_total_kernel,
        [VMEM] * 3,
        [(shape((cols, pairs), F32), VMEM)],
        [],
        0,
        10 * cols * pairs,
    )(txt_a, txt_b, txt_carry)
    across_pieces = img_in // 128
    tiles = back.reshape(n_dp // across_pieces, across_pieces, pieces.shape[1], 128)
    weight_total = tiles.transpose(0, 2, 1, 3).reshape(cols, img_in).astype(F32)
    return weight_total.T, txt_total.T


def solution(mesh):
    n_dp, n_mp = mesh.devices.shape
    sizes = (2, 4, n_dp // 8, 2, n_mp // 2)
    fine = Mesh(mesh.devices.reshape(sizes), AXES)
    placed = (
        P(DP, None),
        P(DP, None),
        P(None, MP),
        P(None, MP),
        P(DP + MP),
        P(DP),
        P(DP, None),
    )
    return jax.shard_map(
        functools.partial(local, sizes),
        mesh=fine,
        in_specs=placed,
        out_specs=(P(None, MP), P(DP, MP)),
        check_vma=False,
    )
```

profile of v0, /device:TPU:24, one launch (start us, length us, event | category | flops | bytes accessed | tf_op | source)
XLA Modules:
  0.0 146.4 jit_solution(12941457921127853316)
XLA Ops:
  0.6 0.7 reduce-precision_convert_fusion.1
  1.3 1.5 %constant_dynamic-slice_fusion = bf16[1024,768]{1,0:T(8,128)(2,1)S(1)} fusion(bf16[2048,768]{1,0:T(8,128)(2,1)} %txt_hbm.3, s32[]{:T(128)S(6)} %select_n.51), kind=kLoop, calls=%fused_computation.24 | loop fusion | bytes 3145732 | tf_op jit(solution)/shard_map/dynamic_slice | solution.py:323
  2.9 0.0 copy-start.6
  2.9 0.0 copy-start.7
  2.9 1.3 pad_maximum_fusion
  4.1 1.9 %collective-permute-start = (bf16[1040,768]{1,0:T(8,128)(2,1)}, bf16[1040,768]{1,0:T(8,128)(2,1)S(1)}, u32[]{:S(2)}, u32[]{:S(2)}) collective-permute-start(bf16[1040,768]{1,0:T(8,128)(2,1)} %pad_maximum_fusion), channel_id=1, source_target_pairs={{0,4},{1,5},{2,6},{3,7},{4,8},{5,9},{6,10},{7,11},{8,12},{9,13},{1... | collective-permute-start | bytes 4792328 | tf_op jit(solution)/shard_map/ppermute | solution.py:304
  6.1 0.0 copy-done.6
  6.1 0.0 copy-done.7
  6.1 0.0 copy-start
  6.1 0.1 collective-permute-start.1
  6.2 0.3 collective-permute-start.2
  6.5 1.8 %collective-permute-done.1.w1 = bf16[192,1792]{1,0:T(8,128)(2,1)S(1)} collective-permute-done((bf16[192,1792]{1,0:T(8,128)(2,1)S(1)}, bf16[192,1792]{1,0:T(8,128)(2,1)S(1)}, u32[]{:S(2)}, u32[]{:S(2)}) %collective-permute-start.1) | collective-permute-done | bytes 688160 | tf_op jit(solution)/shard_map/ppermute | solution.py:304
  8.4 0.0 copy-done
  8.4 0.8 copy-done.1
  9.2 8.6 %shard_map.86 = (f32[384,2048]{1,0:T(8,128)}, f32[2048,384]{1,0:T(8,128)}, f32[1,512]{1,0:T(1,128)}) custom-call(bf16[2048,1024]{1,0:T(8,128)(2,1)} %img_hbm.5, bf16[2048,768]{1,0:T(8,128)(2,1)} %txt_hbm.3, bf16[192,1792]{1,0:T(8,128)(2,1)} %copy-done, bf16[192,1792]{1,0:T(8,128)(2,1)} %copy-done.1, f32[1,512]{1,0:T(1,128)} %bitcast.27), custom_call_target="tpu_custom_call" | custom-call | tf_op jit(solution)/shard_map/pallas_call | solution.py:326
  17.8 0.2 collective-permute-start.4
  18.0 1.3 collective-permute-start.5
  19.3 2.0 %collective-permute-start.6 = (f32[1,512]{1,0:T(1,128)}, f32[1,512]{1,0:T(1,128)S(1)}, u32[]{:S(2)}, u32[]{:S(2)}) collective-permute-start(f32[1,512]{1,0:T(1,128)} %get-tuple-element.23), channel_id=1, source_target_pairs={{0,3},{1,2},{2,1},{3,0},{4,7},{5,6},{6,5},{7,4},{8,11},{9,10},{10,... | collective-permute-start | bytes 6152 | tf_op jit(solution)/shard_map/ppermute | solution.py:304
  21.2 4.2 %collective-permute-done.2.w2 = bf16[192,1792]{1,0:T(8,128)(2,1)} collective-permute-done((bf16[192,1792]{1,0:T(8,128)(2,1)S(1)}, bf16[192,1792]{1,0:T(8,128)(2,1)}, u32[]{:S(2)}, u32[]{:S(2)}) %collective-permute-start.2) | collective-permute-done | bytes 688160 | tf_op jit(solution)/shard_map/ppermute | solution.py:304
  25.5 0.2 collective-permute-start.3
  25.7 0.0 collective-permute-done.4
  25.7 0.7 broadcast_select_fusion.5
  26.4 0.0 collective-permute-done.5
  26.4 0.0 collective-permute-done.6
  26.5 0.6 pad_maximum_fusion.2.er_ref
  27.1 1.0 collective-permute-done.3.w3
  28.1 0.9 copy-done.5
  28.9 38.1 %shard_map.87 = (bf16[768,2048]{1,0:T(8,128)(2,1)}, f32[192,2048]{1,0:T(8,128)}, bf16[768,768]{1,0:T(8,128)(2,1)}, f32[1,2048]{1,0:T(1,128)}, f32[192,2048]{1,0:...) custom-call(bf16[2048,768]{1,0:T(8,128)(2,1)} %txt_hbm.3, f32[2048,384]{1,0:T(8,128)} %get-tuple-element.21.txt_raw_hbm, ...), custom_call_target="tpu_custom_call" | custom-call | tf_op jit(solution)/shard_map/pallas_call | solution.py:350
  67.0 0.0 collective-permute-done.feats
  67.0 0.0 copy-start.3
  67.0 0.2 collective-permute-start.7
  67.2 1.9 %collective-permute-start.8 = (bf16[192,2048]{1,0:T(8,128)(2,1)}, bf16[192,2048]{1,0:T(8,128)(2,1)S(1)}, u32[]{:S(2)}, u32[]{:S(2)}) collective-permute-start(bf16[192,2048]{1,0:T(8,128)(2,1)} %get-tuple-element.35), channel_id=1, source_target_pairs={{0,4},{1,5},{2,6},{3,7},{4,8},{5,9},{6,10},{7,11},{8,12},{9,13},{1... | collective-permute-start | bytes 2359304 | tf_op jit(solution)/shard_map/ppermute | solution.py:304
  69.2 11.4 %shard_map.88 = (f32[192,2048]{1,0:T(8,128)}, f32[1,2048]{1,0:T(1,128)}, f32[192,1024]{1,0:T(8,128)}) custom-call(bf16[1040,768]{1,0:T(8,128)(2,1)} %copy-done.3, bf16[768,768]{1,0:T(8,128)(2,1)} %get-tuple-element.26.wt, bf16[768,2048]{1,0:T(8,128)(2,1)} %get-tuple-element.27.img_emb_hbm, f32[1,2048]{1,0:T(1,128)} %pad_maximum_fusion.2.er_ref, ...), custom_call_target="tpu_custom_call" | custom-call | tf_op jit(solution)/shard_map/pallas_call | solution.py:395
  80.6 0.0 collective-permute-done.7.feats
  80.6 0.0 copy-start.2
  80.6 1.2 copy-done.2
  81.8 14.4 %shard_map.89 = (bf16[64,24,128]{2,1,0:T(8,128)(2,1)}, f32[192,1024]{1,0:T(8,128)}) custom-call(bf16[1040,768]{1,0:T(8,128)(2,1)} %copy-done.2, bf16[768,768]{1,0:T(8,128)(2,1)} %get-tuple-element.26.wt, bf16[768,2048]{1,0:T(8,128)(2,1)} %get-tuple-element.27.img_emb_hbm, f32[1,2048]{1,0:T(1,128)} %pad_maximum_fusion.2.er_ref, ...), custom_call_target="tpu_custom_call" | custom-call | tf_op jit(solution)/shard_map/pallas_call | solution.py:410
  96.2 0.0 collective-permute-done.8.carry
  96.2 0.0 copy-start.4
  96.2 27.5 %all_to_all.10 = bf16[64,24,128]{2,1,0:T(8,128)(2,1)S(1)} all-to-all(bf16[64,24,128]{2,1,0:T(8,128)(2,1)} %get-tuple-element.36), channel_id=1, replica_groups=mesh['yl'=2,'x'=4,'z'=8,'yh'=2,'core'=2] {'yl','x','z'}, dimensions={0} | all-to-all | bytes 786432 | tf_op jit(solution)/shard_map/all_to_all | solution.py:428
  123.7 0.1 reduce_sum.12
  123.8 0.8 broadcast_in_dim.10
  124.6 4.9 %all-to-all-start.1 = ((bf16[64,24,128]{2,1,0:T(8,128)(2,1)}), bf16[64,24,128]{2,1,0:T(8,128)(2,1)S(1)}, u32[]{:S(2)}, u32[]{:S(2)}) async-start(bf16[64,24,128]{2,1,0:T(8,128)(2,1)} %broadcast_in_dim.10), calls=%async_computation.1 | async-start | bytes 786432 | tf_op jit(solution)/shard_map/all_to_all | solution.py:431
  129.5 2.9 %shard_map.90 = f32[192,2048]{1,0:T(8,128)} custom-call(f32[192,1024]{1,0:T(8,128)} %get-tuple-element.37.part_a, f32[192,1024]{1,0:T(8,128)} %get-tuple-element.38.part_b, bf16[192,2048]{1,0:T(8,128)(2,1)} %copy-done.4), custom_call_target="tpu_custom_call" | custom-call | tf_op jit(solution)/shard_map/pallas_call | solution.py:432
  132.4 12.5 %all-to-all-done.1 = bf16[64,24,128]{2,1,0:T(8,128)(2,1)S(1)} async-done(((bf16[64,24,128]{2,1,0:T(8,128)(2,1)}), bf16[64,24,128]{2,1,0:T(8,128)(2,1)S(1)}, u32[]{:S(2)}, u32[]{:S(2)}) %all-to-all-start.1) | async-done | bytes 393248 | tf_op jit(solution)/shard_map/all_to_all | solution.py:431
  144.9 0.1 convert_bitcast_fusion
  145.0 0.1 copy.9
  145.2 1.0 copy.12
  (8 shorter events, 0.1 us)
Async XLA Ops:
  2.9 3.2 %copy-start.6 = (bf16[1024,192]{0,1:T(8,128)(2,1)S(1)}, bf16[1024,192]{0,1:T(8,128)(2,1)}, u32[]{:S(2)}) copy-start(bf16[1024,192]{0,1:T(8,128)(2,1)} %param.9) | copy-start | bytes 1179652
  2.9 3.2 %copy-start.7 = (bf16[768,192]{0,1:T(8,128)(2,1)S(1)}, bf16[768,192]{0,1:T(8,128)(2,1)}, u32[]{:S(2)}) copy-start(bf16[768,192]{0,1:T(8,128)(2,1)} %param.10) | copy-start | bytes 884740
  4.1 62.9 %collective-permute-start = (bf16[1040,768]{1,0:T(8,128)(2,1)}, bf16[1040,768]{1,0:T(8,128)(2,1)S(1)}, u32[]{:S(2)}, u32[]{:S(2)}) collective-permute-start(bf16[1040,768]{1,0:T(8,128)(2,1)} %pad_maximum_fusion), channel_id=1, source_target_pairs={{0,4},{1,5},{2,6},{3,7},{4,8},{5,9},{6,10},{7,11},{8,12},{9,13},{1... | collective-permute-start | bytes 4792328 | tf_op jit(solution)/shard_map/ppermute | solution.py:304
  6.1 2.2 %copy-start = (bf16[192,1792]{1,0:T(8,128)(2,1)}, bf16[192,1792]{1,0:T(8,128)(2,1)S(1)}, u32[]{:S(2)}) copy-start(bf16[192,1792]{1,0:T(8,128)(2,1)S(1)} %pad_maximum_fusion.1.w0) | copy-start | bytes 2064388
  6.1 2.2 %collective-permute-start.1 = (bf16[192,1792]{1,0:T(8,128)(2,1)S(1)}, bf16[192,1792]{1,0:T(8,128)(2,1)S(1)}, u32[]{:S(2)}, u32[]{:S(2)}) collective-permute-start(bf16[192,1792]{1,0:T(8,128)(2,1)S(1)} %pad_maximum_fusion.1.w0), channel_id=1, source_target_pairs={{0,1},{1,0},{2,3},{3,2},{4,5},{5,4},{6,7},{7,6},{8,9},{9,8},{10,11... | collective-permute-start | bytes 2064392 | tf_op jit(solution)/shard_map/ppermute | solution.py:304
  6.2 19.3 %collective-permute-start.2 = (bf16[192,1792]{1,0:T(8,128)(2,1)S(1)}, bf16[192,1792]{1,0:T(8,128)(2,1)}, u32[]{:S(2)}, u32[]{:S(2)}) collective-permute-start(bf16[192,1792]{1,0:T(8,128)(2,1)S(1)} %pad_maximum_fusion.1.w0), channel_id=1, source_target_pairs={{0,130},{1,131},{2,128},{3,129},{4,134},{5,135},{6,132},{7,133},{8... | collective-permute-start | bytes 2064392 | tf_op jit(solution)/shard_map/ppermute | solution.py:304
  8.4 0.8 copy-start.1
  17.8 7.9 %collective-permute-start.4 = (f32[1,512]{1,0:T(1,128)}, f32[1,512]{1,0:T(1,128)S(1)}, u32[]{:S(2)}, u32[]{:S(2)}) collective-permute-start(f32[1,512]{1,0:T(1,128)} %get-tuple-element.23), channel_id=1, source_target_pairs={{0,1},{1,0},{2,3},{3,2},{4,5},{5,4},{6,7},{7,6},{8,9},{9,8},{10,11... | collective-permute-start | bytes 6152 | tf_op jit(solution)/shard_map/ppermute | solution.py:304
  18.0 8.4 %collective-permute-start.5 = (f32[1,512]{1,0:T(1,128)}, f32[1,512]{1,0:T(1,128)S(1)}, u32[]{:S(2)}, u32[]{:S(2)}) collective-permute-start(f32[1,512]{1,0:T(1,128)} %get-tuple-element.23), channel_id=1, source_target_pairs={{0,2},{1,3},{2,0},{3,1},{4,6},{5,7},{6,4},{7,5},{8,10},{9,11},{10,... | collective-permute-start | bytes 6152 | tf_op jit(solution)/shard_map/ppermute | solution.py:304
  19.3 7.2 %collective-permute-start.6 = (f32[1,512]{1,0:T(1,128)}, f32[1,512]{1,0:T(1,128)S(1)}, u32[]{:S(2)}, u32[]{:S(2)}) collective-permute-start(f32[1,512]{1,0:T(1,128)} %get-tuple-element.23), channel_id=1, source_target_pairs={{0,3},{1,2},{2,1},{3,0},{4,7},{5,6},{6,5},{7,4},{8,11},{9,10},{10,... | collective-permute-start | bytes 6152 | tf_op jit(solution)/shard_map/ppermute | solution.py:304
  25.5 2.6 %collective-permute-start.3 = (bf16[192,1792]{1,0:T(8,128)(2,1)}, bf16[192,1792]{1,0:T(8,128)(2,1)S(1)}, u32[]{:S(2)}, u32[]{:S(2)}) collective-permute-start(bf16[192,1792]{1,0:T(8,128)(2,1)} %collective-permute-done.2.w2), channel_id=1, source_target_pairs={{0,1},{1,0},{2,3},{3,2},{4,5},{5,4},{6,7},{7,6},{8,9},{9,8},{10,11... | collective-permute-start | bytes 2064392 | tf_op jit(solution)/shard_map/ppermute | solution.py:304
  28.1 0.9 copy-start.5
  67.0 2.2 %copy-start.3 = (bf16[1040,768]{1,0:T(8,128)(2,1)}, bf16[1040,768]{1,0:T(8,128)(2,1)S(1)}, u32[]{:S(2)}) copy-start(bf16[1040,768]{1,0:T(8,128)(2,1)S(1)} %collective-permute-done.feats) | copy-start | bytes 4792324
  67.0 13.5 %collective-permute-start.7 = (bf16[1040,768]{1,0:T(8,128)(2,1)S(1)}, bf16[1040,768]{1,0:T(8,128)(2,1)S(1)}, u32[]{:S(2)}, u32[]{:S(2)}) collective-permute-start(bf16[1040,768]{1,0:T(8,128)(2,1)S(1)} %collective-permute-done.feats), channel_id=1, source_target_pairs={{0,1},{1,0},{2,3},{3,2},{4,5},{5,4},{6,7},{7,6},{8,9},{9,8},{10,11... | collective-permute-start | bytes 4792328 | tf_op jit(solution)/shard_map/ppermute | solution.py:304
  67.2 28.9 %collective-permute-start.8 = (bf16[192,2048]{1,0:T(8,128)(2,1)}, bf16[192,2048]{1,0:T(8,128)(2,1)S(1)}, u32[]{:S(2)}, u32[]{:S(2)}) collective-permute-start(bf16[192,2048]{1,0:T(8,128)(2,1)} %get-tuple-element.35), channel_id=1, source_target_pairs={{0,4},{1,5},{2,6},{3,7},{4,8},{5,9},{6,10},{7,11},{8,12},{9,13},{1... | collective-permute-start | bytes 2359304 | tf_op jit(solution)/shard_map/ppermute | solution.py:304
  80.6 1.2 copy-start.2
  96.2 33.3 %copy-start.4 = (bf16[192,2048]{1,0:T(8,128)(2,1)}, bf16[192,2048]{1,0:T(8,128)(2,1)S(1)}, u32[]{:S(2)}) copy-start(bf16[192,2048]{1,0:T(8,128)(2,1)S(1)} %collective-permute-done.8.carry) | copy-start | bytes 2359300
  124.6 20.3 %all-to-all-start.1 = ((bf16[64,24,128]{2,1,0:T(8,128)(2,1)}), bf16[64,24,128]{2,1,0:T(8,128)(2,1)S(1)}, u32[]{:S(2)}, u32[]{:S(2)}) async-start(bf16[64,24,128]{2,1,0:T(8,128)(2,1)} %broadcast_in_dim.10), calls=%async_computation.1 | async-start | bytes 786432 | tf_op jit(solution)/shard_map/all_to_all | solution.py:431
where the time goes:
time: 146 us
  Pallas kernels  75.3 us (52%)
  blocking collectives  27.5 us (19%)
  waiting for transfers between devices  19.6 us (13%)
  starting transfers between devices  13 us (9%)
  local copies, waits for them, and re-layouts  6.39 us (4%)
  other arithmetic  3.47 us (2%)
    pallas_call x1, Pallas kernels, local(): call(first_kernel, [ANY] * 4 + [VMEM] * 7, [(shape((width, pairs), BF), A...  38.1 us
    all_to_all x1, blocking collectives, local(): got = lax.all_to_all(pieces, DP, 0, 0, tiled=True)  27.5 us
    pallas_call x1, Pallas kernels, local(): call(last_kernel, [VMEM, VMEM, ANY, VMEM, ANY, VMEM, ANY, VMEM, ANY], [(s...  14.4 us
    all_to_all x1, waiting for transfers between devices, local(): back = lax.all_to_all(spread, DP, 0, 0, tiled=True)  12.5 us
    pallas_call x1, Pallas kernels, local(): call(second_kernel, [VMEM, VMEM, ANY, VMEM, ANY, VMEM], [(shape((cols, pa...  11.4 us
    pallas_call x1, Pallas kernels, local(): call(near_kernel, [ANY, ANY, VMEM, VMEM, VMEM], [(shape((2 * cols, pairs)...  8.58 us
    ppermute x9, starting transfers between devices, send(): return lax.ppermute(a, AXES, route)  8.17 us
    ppermute x9, waiting for transfers between devices, send(): return lax.ppermute(a, AXES, route)  7.07 us
  transfers between devices with their start and end apart: 10, of which 4 were waited for; matrix products, arithmetic and copies ran while one was open for 1% of the time, Pallas kernels for 51%

commit v1 on v0

--- a/solution.py
+++ b/solution.py
@@ -19,7 +19,7 @@
 BF = jnp.bfloat16
 F32 = jnp.float32
 VMEM_LIMIT = 56 * 1024 * 1024
-TXT_CHUNK, IMG_CHUNK = 512, 1024
+TXT_CHUNK, IMG_CHUNK = 512, 256
 
 NT = (((1,), (1,)), ((), ()))
 NN = (((1,), (0,)), ((), ()))
@@ -72,25 +72,60 @@
     return made
 
 
+def parcel_kernel(txt_hbm, lse_ref, wi_hbm, wt_hbm, out_ref, w_ref, sems):
+    rows = out_ref.shape[0] - lse_ref.shape[0]
+    depth = wi_hbm.shape[1]
+    first = pl.multiple_of(lax.axis_index("core") * rows, rows)
+    loads = copies(
+        [
+            (wi_hbm, w_ref.at[:, pl.ds(0, depth)]),
+            (wt_hbm, w_ref.at[:, pl.ds(depth, wt_hbm.shape[1])]),
+            (txt_hbm.at[pl.ds(first, rows), :], out_ref.at[pl.ds(0, rows), :]),
+        ],
+        sems,
+    )
+    lse = lse_ref[...]
+    high = lse.astype(BF)
+    rest = lse - high.astype(F32)
+    middle = rest.astype(BF)
+    low = (rest - middle.astype(F32)).astype(BF)
+    for n, part in enumerate((high, middle, low)):
+        out_ref[rows:, n * 128 : (n + 1) * 128] = part
+    out_ref[rows:, 384:] = jnp.zeros((lse.shape[0], out_ref.shape[1] - 384), BF)
+    for c in loads:
+        c.wait()
+
+
+def row_blocks(pairs):
+    return [pl.ds(r, pairs // 4) for r in range(0, pairs, pairs // 4)]
+
+
 def near_kernel(
     img_hbm, txt_hbm, w0, w1, row_ref,
     img_raw, txt_raw, er_ref,
     img_s, txt_s, wi_s, wt_s, sems,
 ):
-    txt_in, img_in = copies([(txt_hbm, txt_s), (img_hbm, img_s)], sems)
+    pairs, depth = img_s.shape
+    block = pairs // 4
+    blocks = row_blocks(pairs)
+    loads = copies(
+        [(txt_hbm.at[b, :], txt_s.at[b, :]) for b in blocks]
+        + [(img_hbm.at[b, :], img_s.at[b, :]) for b in blocks],
+        sems,
+    )
     er_ref[...] = loss_weight * jnp.exp(-row_ref[...])
     cols = w0.shape[0]
-    depth = wi_s.shape[1]
     for n, w in enumerate((w0, w1)):
         wi_s[n * cols : (n + 1) * cols, :] = w[:, 0:depth]
         wt_s[n * cols : (n + 1) * cols, :] = w[:, depth:]
-    pairs = img_s.shape[0]
-    txt_in.wait()
-    for r in range(0, pairs, 512):
-        txt_raw[r : r + 512, :] = dot(txt_s[r : r + 512, :], wt_s[...], NT)
-    img_in.wait()
-    for r in range(0, pairs, 512):
-        img_raw[:, r : r + 512] = dot(wi_s[...], img_s[r : r + 512, :], NT)
+    for n in range(4):
+        at = slice(n * block, (n + 1) * block)
+        loads[n].wait()
+        txt_raw[at, :] = dot(txt_s[at, :], wt_s[...], NT)
+    for n in range(4):
+        at = slice(n * block, (n + 1) * block)
+        loads[4 + n].wait()
+        img_raw[:, at] = dot(wi_s[...], img_s[at, :], NT)
 
 
 def stand(lse_ref, first, column_ref):
@@ -99,28 +134,22 @@
         column_ref[n * 128 : (n + 1) * 128, :] = jnp.transpose(jnp.broadcast_to(weight, (128, 128)))
 
 
-def score_tile(
-    txt_emb, txt_own_t, img_emb_t, er_ref, ec_s, label_ref, g_s, finish, txt_chunk, img_chunk
-):
+def score_tile(txt_emb, txt_own_t, img_emb_t, er_ref, ec_s, label_ref, g_s, finish):
     texts = txt_emb.shape[0]
-    images = img_emb_t.shape[1]
-    cols = txt_own_t.shape[0]
-    for i in range(0, images, img_chunk):
-        at = slice(i, i + img_chunk)
-        img_part = jnp.zeros((cols, img_chunk), F32)
-        along = jnp.zeros((1, img_chunk), F32)
+    for i in range(0, img_emb_t.shape[1], IMG_CHUNK):
+        at = slice(i, i + IMG_CHUNK)
+        along = jnp.zeros((1, IMG_CHUNK), F32)
         er = er_ref[:, at]
-        for t in range(0, texts, txt_chunk):
-            raw = dot(txt_emb[t : t + txt_chunk, :], img_emb_t[:, at], NN)
-            g = jnp.exp2(raw * exp_scale) * (er + ec_s[t : t + txt_chunk, 0:1])
+        for t in range(0, texts, TXT_CHUNK):
+            raw = dot(txt_emb[t : t + TXT_CHUNK, :], img_emb_t[:, at], NN)
+            g = jnp.exp2(raw * exp_scale) * (er + ec_s[t : t + TXT_CHUNK, 0:1])
             if label_ref is not None:
-                place = lax.broadcasted_iota(jnp.int32, (txt_chunk, img_chunk), 0)
+                place = lax.broadcasted_iota(jnp.int32, (TXT_CHUNK, IMG_CHUNK), 0)
                 g = g - jnp.where(place == (label_ref[:, at] - t), 2.0 * loss_weight, 0.0)
             g = g.astype(BF)
             along = along + jnp.sum(g.astype(F32) * raw, 0, keepdims=True)
-            img_part = img_part + dot(txt_own_t[:, t : t + txt_chunk], g, NN)
-            g_s[t : t + txt_chunk, at] = g
-        finish(at, img_part, along)
+            g_s[t : t + TXT_CHUNK, at] = g
+        finish(at, dot(txt_own_t[...], g_s[:, at], NN), along)
 
 
 def text_part(g_s, img_emb_t, cols, out_ref):
@@ -136,9 +165,15 @@
     txt_s, txt_raw, img_s, img_raw, wi_s, wt_s, txt_emb, txt_own_t, img_emb_t, img_own_t, ec_s, g_s,
     sems, out_sems,
 ):
-    loads = copies(
-        [(txt_hbm, txt_s), (txt_raw_hbm, txt_raw), (img_hbm, img_s), (img_raw_hbm, img_raw)], sems
-    )
+    pairs = txt_s.shape[0]
+    block = pairs // 4
+    blocks = row_blocks(pairs)
+    moves = []
+    for b in blocks:
+        moves += [(txt_hbm.at[b, :], txt_s.at[b, :]), (txt_raw_hbm.at[b, :], txt_raw.at[b, :])]
+    for b in blocks:
+        moves += [(img_hbm.at[b, :], img_s.at[b, :]), (img_raw_hbm.at[:, b], img_raw.at[:, b])]
+    loads = copies(moves, sems)
     cols = w0.shape[0]
     depth = wi_s.shape[1]
     for n, w in enumerate((w0, w1, w2, w3)):
@@ -148,23 +183,22 @@
     stand(col_ref, 0, ec_s)
     save_wt = pltpu.make_async_copy(wt_s, wt_hbm, out_sems.at[0])
     save_wt.start()
-    pairs = txt_s.shape[0]
     two = 2 * cols
-    loads[0].wait()
-    loads[1].wait()
-    for r in range(0, pairs, 512):
-        far = dot(txt_s[r : r + 512, :], wt_s[two:, :], NT)
-        near = txt_raw[r : r + 512, :]
+    for n, r in enumerate(range(0, pairs, block)):
+        loads[2 * n].wait()
+        loads[2 * n + 1].wait()
+        far = dot(txt_s[r : r + block, :], wt_s[two:, :], NT)
+        near = txt_raw[r : r + block, :]
         total = jnp.sum(near * near, -1, keepdims=True) + jnp.sum(far * far, -1, keepdims=True)
         inv = lax.rsqrt(total + epsilon)
         near = near * inv
-        txt_emb[r : r + 512, 0:two] = near.astype(BF)
-        txt_emb[r : r + 512, two:] = (far * inv).astype(BF)
-        txt_own_t[:, r : r + 512] = jnp.transpose(near[:, 0:256])[0:cols, :].astype(BF)
-    loads[2].wait()
-    loads[3].wait()
-    for r in range(0, pairs, 512):
-        at = slice(r, r + 512)
+        txt_emb[r : r + block, 0:two] = near.astype(BF)
+        txt_emb[r : r + block, two:] = (far * inv).astype(BF)
+        txt_own_t[:, r : r + block] = jnp.transpose(near[:, 0:256])[0:cols, :].astype(BF)
+    for n, r in enumerate(range(0, pairs, block)):
+        at = slice(r, r + block)
+        loads[8 + 2 * n].wait()
+        loads[9 + 2 * n].wait()
         far = dot(wi_s[...], img_s[at, :], NT)
         near = img_raw[:, at]
         total = jnp.sum(near * near, 0, keepdims=True) + jnp.sum(far * far, 0, keepdims=True)
@@ -185,9 +219,7 @@
         img_part_ref[:, at] = img_part
         along_ref[:, at] = along
 
-    score_tile(
-        txt_emb, txt_own_t, img_emb_t, er_ref, ec_s, label_ref, g_s, finish, TXT_CHUNK, IMG_CHUNK
-    )
+    score_tile(txt_emb, txt_own_t, img_emb_t, er_ref, ec_s, label_ref, g_s, finish)
     text_part(g_s, img_emb_t, cols, txt_part_ref)
     save_wt.wait()
     for c in saves:
@@ -218,16 +250,15 @@
     loads = copies([(img_emb_hbm, img_emb_t), (img_part_hbm, img_part_s)], sems)
     stand_half(feats, lax.axis_index("core"), lse_s, ec_s)
     project_texts(feats, wt, txt_emb, txt_own_t)
-    for c in loads:
-        c.wait()
+    loads[0].wait()
 
     def finish(at, img_part, along):
+        if at.start == 0:
+            loads[1].wait()
         img_part_ref[:, at] = img_part_s[:, at] + img_part
         along_ref[:, at] = along_in[:, at] + along
 
-    score_tile(
-        txt_emb, txt_own_t, img_emb_t, er_ref, ec_s, None, g_s, finish, TXT_CHUNK, IMG_CHUNK
-    )
+    score_tile(txt_emb, txt_own_t, img_emb_t, er_ref, ec_s, None, g_s, finish)
     text_part(g_s, img_emb_t, txt_own_t.shape[0], txt_part_ref)
 
 
@@ -245,19 +276,20 @@
     )
     stand_half(feats, 1 - lax.axis_index("core"), lse_s, ec_s)
     project_texts(feats, wt, txt_emb, txt_own_t)
-    for c in loads:
-        c.wait()
+    loads[0].wait()
 
     def finish(at, img_part, along):
+        if at.start == 0:
+            loads[1].wait()
+            loads[2].wait()
         grad = img_part_s[:, at] + img_part
         toward = along_in[:, at] + along
         d_raw[:, at] = (
             (grad - img_own_t[:, at] * toward) * (scale_logit * inv_ref[:, at])
         ).astype(BF)
 
-    score_tile(
-        txt_emb, txt_own_t, img_emb_t, er_ref, ec_s, None, g_s, finish, TXT_CHUNK, IMG_CHUNK
-    )
+    score_tile(txt_emb, txt_own_t, img_emb_t, er_ref, ec_s, None, g_s, finish)
+    loads[3].wait()
     n_pieces, rb, cb = pieces_ref.shape
     across = img_s.shape[1] // cb
     for k in range(0, img_s.shape[1], 256):
@@ -310,19 +342,22 @@
 
     shape = jax.ShapeDtypeStruct
     half = pairs // n_core
-    w_own = jnp.concatenate([img_weight.T, txt_weight.T], 1)
+    lse = col_lse.reshape(pairs // 128, 128)
+    parcel, w_own = call(
+        parcel_kernel,
+        [ANY, VMEM, ANY, ANY],
+        [
+            (shape((half + lse.shape[0], txt_in), BF), VMEM),
+            (shape((cols, img_in + txt_in), BF), VMEM),
+        ],
+        [pltpu.SemaphoreType.DMA((3,))],
+        0,
+        0,
+    )(txt_feats, lse, img_weight.T, txt_weight.T)
+    feats_a = send(parcel, onward)
     w_far = send(w_own, across)
     w_near = send(w_own, swap)
     w_far_near = send(w_far, swap)
-    lse = col_lse.reshape(pairs // 128, 128)
-    high = lax.reduce_precision(lse, 8, 7)
-    middle = lax.reduce_precision(lse - high, 8, 7)
-    low = (lse - high) - middle
-    lse_rows = jnp.concatenate([high, middle, low], 1).astype(BF)
-    lse_rows = jnp.pad(lse_rows, ((0, 0), (0, txt_in - 3 * 128)))
-    mine = lax.dynamic_slice_in_dim(txt_feats, core * half, half, 0)
-    feats_a = send(jnp.concatenate([mine, lse_rows], 0), onward)
-
     img_raw, txt_raw, er_own = call(
         near_kernel,
         [ANY, ANY, VMEM, VMEM, VMEM],
@@ -336,7 +371,7 @@
             pltpu.VMEM((pairs, txt_in), BF),
             pltpu.VMEM((2 * cols, img_in), BF),
             pltpu.VMEM((2 * cols, txt_in), BF),
-            pltpu.SemaphoreType.DMA((2,)),
+            pltpu.SemaphoreType.DMA((8,)),
         ],
         2 * pairs * 2 * cols * (img_in + txt_in),
         2 * pairs * (img_in + txt_in + 2 * width),
@@ -372,7 +407,7 @@
             pltpu.VMEM((cols, pairs), F32),
             pltpu.VMEM((pairs, 128), F32),
             pltpu.VMEM((pairs, pairs), BF),
-            pltpu.SemaphoreType.DMA((4,)),
+            pltpu.SemaphoreType.DMA((16,)),
             pltpu.SemaphoreType.DMA((3,)),
         ],
         tile_flops,

time: 146 us -> 144 us (0.986)
  Pallas kernels: 75.3 us -> 77.6 us
  other arithmetic: 3.47 us -> 1.45 us
  local copies, waits for them, and re-layouts: 6.39 us -> 4.86 us
    pallas_call x0 -> x1, Pallas kernels: none -> 3.69 us  [local(): call(parcel_kernel, [ANY, VMEM, ANY, ANY], [(shape((half + lse.shape[0],...]
    pallas_call x1, Pallas kernels: 14.4 us -> 12.7 us  [local(): call(last_kernel, [VMEM, VMEM, ANY, VMEM, ANY, VMEM, ANY, VMEM, ANY], [(s...]
    dynamic_slice x1 -> x0, local copies, waits for them, and re-layouts: 1.51 us -> none  [local(): mine = lax.dynamic_slice_in_dim(txt_feats, core * half, half, 0)]
    unnamed x17 -> x13, local copies, waits for them, and re-layouts: 3.94 us -> 3.92 us
where the time goes in v1:
time: 144 us
  Pallas kernels  77.6 us (54%)
  blocking collectives  27.5 us (19%)
  waiting for transfers between devices  18.7 us (13%)
  starting transfers between devices  12.9 us (9%)
  local copies, waits for them, and re-layouts  4.86 us (3%)
  other arithmetic  1.45 us (1%)
    pallas_call x1, Pallas kernels, local(): call(first_kernel, [ANY] * 4 + [VMEM] * 7, [(shape((width, pairs), BF), A...  37.2 us
    all_to_all x1, blocking collectives, local(): got = lax.all_to_all(pieces, DP, 0, 0, tiled=True)  27.5 us
    pallas_call x1, Pallas kernels, local(): call(last_kernel, [VMEM, VMEM, ANY, VMEM, ANY, VMEM, ANY, VMEM, ANY], [(s...  12.7 us
    all_to_all x1, waiting for transfers between devices, local(): back = lax.all_to_all(spread, DP, 0, 0, tiled=True)  12.5 us
    pallas_call x1, Pallas kernels, local(): call(second_kernel, [VMEM, VMEM, ANY, VMEM, ANY, VMEM], [(shape((cols, pa...  11.7 us
    pallas_call x1, Pallas kernels, local(): call(near_kernel, [ANY, ANY, VMEM, VMEM, VMEM], [(shape((2 * cols, pairs)...  9.42 us
    ppermute x9, starting transfers between devices, send(): return lax.ppermute(a, AXES, route)  8.07 us
    ppermute x9, waiting for transfers between devices, send(): return lax.ppermute(a, AXES, route)  6.18 us
  transfers between devices with their start and end apart: 10, of which 4 were waited for; matrix products, arithmetic and copies ran while one was open for 1% of the time, Pallas kernels for 51%

profile of v1, /device:TPU:24, one launch (start us, length us, event | category | flops | bytes accessed | tf_op | source)
XLA Modules:
  0.0 144.1 jit_solution(18394474436411077782)
XLA Ops:
  0.6 3.7 %shard_map.86 = (bf16[1040,768]{1,0:T(8,128)(2,1)}, bf16[192,1792]{1,0:T(8,128)(2,1)}) custom-call(bf16[2048,768]{1,0:T(8,128)(2,1)} %txt_hbm.5, f32[16,128]{1,0:T(8,128)} %bitcast.23, bf16[192,1024]{1,0:T(8,128)(2,1)} %bitcast.21, bf16[192,768]{1,0:T(8,128)(2,1)} %bitcast.22), custom_call_target="tpu_custom_call" | custom-call | tf_op jit(solution)/shard_map/pallas_call | solution.py:346
  4.3 2.0 %collective-permute-start = (bf16[1040,768]{1,0:T(8,128)(2,1)}, bf16[1040,768]{1,0:T(8,128)(2,1)S(1)}, u32[]{:S(2)}, u32[]{:S(2)}) collective-permute-start(bf16[1040,768]{1,0:T(8,128)(2,1)} %get-tuple-element.23), channel_id=1, source_target_pairs={{0,4},{1,5},{2,6},{3,7},{4,8},{5,9},{6,10},{7,11},{8,12},{9,13},{1... | collective-permute-start | bytes 4792328 | tf_op jit(solution)/shard_map/ppermute | solution.py:336
  6.3 0.0 collective-permute-start.1
  6.3 0.2 collective-permute-start.2
  6.6 2.1 %collective-permute-done.1.w1 = bf16[192,1792]{1,0:T(8,128)(2,1)S(1)} collective-permute-done((bf16[192,1792]{1,0:T(8,128)(2,1)}, bf16[192,1792]{1,0:T(8,128)(2,1)S(1)}, u32[]{:S(2)}, u32[]{:S(2)}) %collective-permute-start.1) | collective-permute-done | bytes 688160 | tf_op jit(solution)/shard_map/ppermute | solution.py:336
  8.7 0.0 copy-start
  8.7 0.9 copy-done
  9.5 9.4 %shard_map.87 = (f32[384,2048]{1,0:T(8,128)}, f32[2048,384]{1,0:T(8,128)}, f32[1,512]{1,0:T(1,128)}) custom-call(bf16[2048,1024]{1,0:T(8,128)(2,1)} %img_hbm.5, bf16[2048,768]{1,0:T(8,128)(2,1)} %txt_hbm.5, bf16[192,1792]{1,0:T(8,128)(2,1)} %get-tuple-element.24.w0, bf16[192,1792]{1,0:T(8,128)(2,1)} %copy-done, f32[1,512]{1,0:T(1,128)} %bitcast.25), custom_call_target="tpu_custom_call" | custom-call | tf_op jit(solution)/shard_map/pallas_call | solution.py:361
  19.0 0.2 collective-permute-start.4
  19.2 1.2 collective-permute-start.5
  20.4 2.0 %collective-permute-start.6 = (f32[1,512]{1,0:T(1,128)}, f32[1,512]{1,0:T(1,128)S(1)}, u32[]{:S(2)}, u32[]{:S(2)}) collective-permute-start(f32[1,512]{1,0:T(1,128)} %get-tuple-element.27), channel_id=1, source_target_pairs={{0,3},{1,2},{2,1},{3,0},{4,7},{5,6},{6,5},{7,4},{8,11},{9,10},{10,... | collective-permute-start | bytes 6152 | tf_op jit(solution)/shard_map/ppermute | solution.py:336
  22.4 3.3 %collective-permute-done.2.w2 = bf16[192,1792]{1,0:T(8,128)(2,1)S(1)} collective-permute-done((bf16[192,1792]{1,0:T(8,128)(2,1)}, bf16[192,1792]{1,0:T(8,128)(2,1)S(1)}, u32[]{:S(2)}, u32[]{:S(2)}) %collective-permute-start.2) | collective-permute-done | bytes 688160 | tf_op jit(solution)/shard_map/ppermute | solution.py:336
  25.7 0.0 copy-start.4
  25.7 0.2 collective-permute-start.3
  25.9 0.0 collective-permute-done.4
  25.9 0.7 broadcast_select_fusion.5
  26.6 0.0 collective-permute-done.5
  26.6 0.0 collective-permute-done.6
  26.7 0.6 pad_maximum_fusion.er_ref
  27.3 0.8 collective-permute-done.3.w3
  28.1 0.0 copy-start.5
  28.1 0.0 copy-done.4
  28.1 0.9 copy-done.5
  28.9 37.2 %shard_map.88 = (bf16[768,2048]{1,0:T(8,128)(2,1)}, f32[192,2048]{1,0:T(8,128)}, bf16[768,768]{1,0:T(8,128)(2,1)}, f32[1,2048]{1,0:T(1,128)}, f32[192,2048]{1,0:...) custom-call(bf16[2048,768]{1,0:T(8,128)(2,1)} %txt_hbm.5, f32[2048,384]{1,0:T(8,128)} %get-tuple-element.25.txt_raw_hbm, ...), custom_call_target="tpu_custom_call" | custom-call | tf_op jit(solution)/shard_map/pallas_call | solution.py:385
  66.1 0.0 collective-permute-done.feats
  66.1 0.0 copy-start.2
  66.1 0.2 collective-permute-start.7
  66.3 1.9 %collective-permute-start.8 = (bf16[192,2048]{1,0:T(8,128)(2,1)}, bf16[192,2048]{1,0:T(8,128)(2,1)S(1)}, u32[]{:S(2)}, u32[]{:S(2)}) collective-permute-start(bf16[192,2048]{1,0:T(8,128)(2,1)} %get-tuple-element.39), channel_id=1, source_target_pairs={{0,4},{1,5},{2,6},{3,7},{4,8},{5,9},{6,10},{7,11},{8,12},{9,13},{1... | collective-permute-start | bytes 2359304 | tf_op jit(solution)/shard_map/ppermute | solution.py:336
  68.3 0.0 copy-done.2
  68.3 11.7 %shard_map.89 = (f32[192,2048]{1,0:T(8,128)}, f32[1,2048]{1,0:T(1,128)}, f32[192,1024]{1,0:T(8,128)}) custom-call(bf16[1040,768]{1,0:T(8,128)(2,1)} %copy-done.2, bf16[768,768]{1,0:T(8,128)(2,1)} %get-tuple-element.30.wt, bf16[768,2048]{1,0:T(8,128)(2,1)} %get-tuple-element.31.img_emb_hbm, f32[1,2048]{1,0:T(1,128)} %pad_maximum_fusion.er_ref, ...), custom_call_target="tpu_custom_call" | custom-call | tf_op jit(solution)/shard_map/pallas_call | solution.py:430
  80.0 0.0 collective-permute-done.7.feats
  80.0 0.0 copy-start.1
  80.0 1.2 copy-done.1
  81.2 12.7 %shard_map.90 = (bf16[64,24,128]{2,1,0:T(8,128)(2,1)}, f32[192,1024]{1,0:T(8,128)}) custom-call(bf16[1040,768]{1,0:T(8,128)(2,1)} %copy-done.1, bf16[768,768]{1,0:T(8,128)(2,1)} %get-tuple-element.30.wt, bf16[768,2048]{1,0:T(8,128)(2,1)} %get-tuple-element.31.img_emb_hbm, f32[1,2048]{1,0:T(1,128)} %pad_maximum_fusion.er_ref, ...), custom_call_target="tpu_custom_call" | custom-call | tf_op jit(solution)/shard_map/pallas_call | solution.py:445
  93.9 0.0 collective-permute-done.8.carry
  93.9 0.0 copy-start.3
  93.9 27.5 %all_to_all.10 = bf16[64,24,128]{2,1,0:T(8,128)(2,1)S(1)} all-to-all(bf16[64,24,128]{2,1,0:T(8,128)(2,1)} %get-tuple-element.40), channel_id=1, replica_groups=mesh['yl'=2,'x'=4,'z'=8,'yh'=2,'core'=2] {'yl','x','z'}, dimensions={0} | all-to-all | bytes 786432 | tf_op jit(solution)/shard_map/all_to_all | solution.py:463
  121.5 0.1 reduce_sum.12
  121.6 0.8 broadcast_in_dim.10
  122.4 4.9 %all-to-all-start.1 = ((bf16[64,24,128]{2,1,0:T(8,128)(2,1)}), bf16[64,24,128]{2,1,0:T(8,128)(2,1)S(1)}, u32[]{:S(2)}, u32[]{:S(2)}) async-start(bf16[64,24,128]{2,1,0:T(8,128)(2,1)} %broadcast_in_dim.10), calls=%async_computation.1 | async-start | bytes 786432 | tf_op jit(solution)/shard_map/all_to_all | solution.py:466
  127.3 0.0 copy-done.3
  127.3 2.9 %shard_map.91 = f32[192,2048]{1,0:T(8,128)} custom-call(f32[192,1024]{1,0:T(8,128)} %get-tuple-element.41.part_a, f32[192,1024]{1,0:T(8,128)} %get-tuple-element.42.part_b, bf16[192,2048]{1,0:T(8,128)(2,1)} %copy-done.3), custom_call_target="tpu_custom_call" | custom-call | tf_op jit(solution)/shard_map/pallas_call | solution.py:467
  130.2 12.5 %all-to-all-done.1 = bf16[64,24,128]{2,1,0:T(8,128)(2,1)S(1)} async-done(((bf16[64,24,128]{2,1,0:T(8,128)(2,1)}), bf16[64,24,128]{2,1,0:T(8,128)(2,1)S(1)}, u32[]{:S(2)}, u32[]{:S(2)}) %all-to-all-start.1) | async-done | bytes 393248 | tf_op jit(solution)/shard_map/all_to_all | solution.py:466
  142.7 0.1 convert_bitcast_fusion
  142.7 0.1 copy.9
  142.9 1.0 copy.12
  (2 shorter events, 0.0 us)
Async XLA Ops:
  4.3 61.8 %collective-permute-start = (bf16[1040,768]{1,0:T(8,128)(2,1)}, bf16[1040,768]{1,0:T(8,128)(2,1)S(1)}, u32[]{:S(2)}, u32[]{:S(2)}) collective-permute-start(bf16[1040,768]{1,0:T(8,128)(2,1)} %get-tuple-element.23), channel_id=1, source_target_pairs={{0,4},{1,5},{2,6},{3,7},{4,8},{5,9},{6,10},{7,11},{8,12},{9,13},{1... | collective-permute-start | bytes 4792328 | tf_op jit(solution)/shard_map/ppermute | solution.py:336
  6.3 2.4 %collective-permute-start.1 = (bf16[192,1792]{1,0:T(8,128)(2,1)}, bf16[192,1792]{1,0:T(8,128)(2,1)S(1)}, u32[]{:S(2)}, u32[]{:S(2)}) collective-permute-start(bf16[192,1792]{1,0:T(8,128)(2,1)} %get-tuple-element.24.w0), channel_id=1, source_target_pairs={{0,1},{1,0},{2,3},{3,2},{4,5},{5,4},{6,7},{7,6},{8,9},{9,8},{10,11... | collective-permute-start | bytes 2064392 | tf_op jit(solution)/shard_map/ppermute | solution.py:336
  6.3 19.4 %collective-permute-start.2 = (bf16[192,1792]{1,0:T(8,128)(2,1)}, bf16[192,1792]{1,0:T(8,128)(2,1)S(1)}, u32[]{:S(2)}, u32[]{:S(2)}) collective-permute-start(bf16[192,1792]{1,0:T(8,128)(2,1)} %get-tuple-element.24.w0), channel_id=1, source_target_pairs={{0,130},{1,131},{2,128},{3,129},{4,134},{5,135},{6,132},{7,133},{8... | collective-permute-start | bytes 2064392 | tf_op jit(solution)/shard_map/ppermute | solution.py:336
  8.7 0.9 copy-start
  19.0 7.0 %collective-permute-start.4 = (f32[1,512]{1,0:T(1,128)}, f32[1,512]{1,0:T(1,128)S(1)}, u32[]{:S(2)}, u32[]{:S(2)}) collective-permute-start(f32[1,512]{1,0:T(1,128)} %get-tuple-element.27), channel_id=1, source_target_pairs={{0,1},{1,0},{2,3},{3,2},{4,5},{5,4},{6,7},{7,6},{8,9},{9,8},{10,11... | collective-permute-start | bytes 6152 | tf_op jit(solution)/shard_map/ppermute | solution.py:336
  19.2 7.5 %collective-permute-start.5 = (f32[1,512]{1,0:T(1,128)}, f32[1,512]{1,0:T(1,128)S(1)}, u32[]{:S(2)}, u32[]{:S(2)}) collective-permute-start(f32[1,512]{1,0:T(1,128)} %get-tuple-element.27), channel_id=1, source_target_pairs={{0,2},{1,3},{2,0},{3,1},{4,6},{5,7},{6,4},{7,5},{8,10},{9,11},{10,... | collective-permute-start | bytes 6152 | tf_op jit(solution)/shard_map/ppermute | solution.py:336
  20.4 6.2 %collective-permute-start.6 = (f32[1,512]{1,0:T(1,128)}, f32[1,512]{1,0:T(1,128)S(1)}, u32[]{:S(2)}, u32[]{:S(2)}) collective-permute-start(f32[1,512]{1,0:T(1,128)} %get-tuple-element.27), channel_id=1, source_target_pairs={{0,3},{1,2},{2,1},{3,0},{4,7},{5,6},{6,5},{7,4},{8,11},{9,10},{10,... | collective-permute-start | bytes 6152 | tf_op jit(solution)/shard_map/ppermute | solution.py:336
  25.7 2.4 %copy-start.4 = (bf16[192,1792]{1,0:T(8,128)(2,1)}, bf16[192,1792]{1,0:T(8,128)(2,1)S(1)}, u32[]{:S(2)}) copy-start(bf16[192,1792]{1,0:T(8,128)(2,1)S(1)} %collective-permute-done.2.w2) | copy-start | bytes 2064388
  25.7 2.4 %collective-permute-start.3 = (bf16[192,1792]{1,0:T(8,128)(2,1)S(1)}, bf16[192,1792]{1,0:T(8,128)(2,1)S(1)}, u32[]{:S(2)}, u32[]{:S(2)}) collective-permute-start(bf16[192,1792]{1,0:T(8,128)(2,1)S(1)} %collective-permute-done.2.w2), channel_id=1, source_target_pairs={{0,1},{1,0},{2,3},{3,2},{4,5},{5,4},{6,7},{7,6},{8,9},{9,8},{10,11... | collective-permute-start | bytes 2064392 | tf_op jit(solution)/shard_map/ppermute | solution.py:336
  28.1 0.9 copy-start.5
  66.1 2.2 %copy-start.2 = (bf16[1040,768]{1,0:T(8,128)(2,1)}, bf16[1040,768]{1,0:T(8,128)(2,1)S(1)}, u32[]{:S(2)}) copy-start(bf16[1040,768]{1,0:T(8,128)(2,1)S(1)} %collective-permute-done.feats) | copy-start | bytes 4792324
  66.1 13.9 %collective-permute-start.7 = (bf16[1040,768]{1,0:T(8,128)(2,1)S(1)}, bf16[1040,768]{1,0:T(8,128)(2,1)S(1)}, u32[]{:S(2)}, u32[]{:S(2)}) collective-permute-start(bf16[1040,768]{1,0:T(8,128)(2,1)S(1)} %collective-permute-done.feats), channel_id=1, source_target_pairs={{0,1},{1,0},{2,3},{3,2},{4,5},{5,4},{6,7},{7,6},{8,9},{9,8},{10,11... | collective-permute-start | bytes 4792328 | tf_op jit(solution)/shard_map/ppermute | solution.py:336
  66.3 27.6 %collective-permute-start.8 = (bf16[192,2048]{1,0:T(8,128)(2,1)}, bf16[192,2048]{1,0:T(8,128)(2,1)S(1)}, u32[]{:S(2)}, u32[]{:S(2)}) collective-permute-start(bf16[192,2048]{1,0:T(8,128)(2,1)} %get-tuple-element.39), channel_id=1, source_target_pairs={{0,4},{1,5},{2,6},{3,7},{4,8},{5,9},{6,10},{7,11},{8,12},{9,13},{1... | collective-permute-start | bytes 2359304 | tf_op jit(solution)/shard_map/ppermute | solution.py:336
  80.0 1.2 copy-start.1
  93.9 33.3 %copy-start.3 = (bf16[192,2048]{1,0:T(8,128)(2,1)}, bf16[192,2048]{1,0:T(8,128)(2,1)S(1)}, u32[]{:S(2)}) copy-start(bf16[192,2048]{1,0:T(8,128)(2,1)S(1)} %collective-permute-done.8.carry) | copy-start | bytes 2359300
  122.4 20.3 %all-to-all-start.1 = ((bf16[64,24,128]{2,1,0:T(8,128)(2,1)}), bf16[64,24,128]{2,1,0:T(8,128)(2,1)S(1)}, u32[]{:S(2)}, u32[]{:S(2)}) async-start(bf16[64,24,128]{2,1,0:T(8,128)(2,1)} %broadcast_in_dim.10), calls=%async_computation.1 | async-start | bytes 786432 | tf_op jit(solution)/shard_map/all_to_all | solution.py:466

commit v2 on v1

--- a/solution.py
+++ b/solution.py
@@ -80,7 +80,10 @@
         [
             (wi_hbm, w_ref.at[:, pl.ds(0, depth)]),
             (wt_hbm, w_ref.at[:, pl.ds(depth, wt_hbm.shape[1])]),
-            (txt_hbm.at[pl.ds(first, rows), :], out_ref.at[pl.ds(0, rows), :]),
+        ]
+        + [
+            (txt_hbm.at[pl.ds(first + r, rows // 8), :], out_ref.at[pl.ds(r, rows // 8), :])
+            for r in range(0, rows, rows // 8)
         ],
         sems,
     )
@@ -159,11 +162,18 @@
         ).astype(out_ref.dtype)
 
 
+def save_strip(src, dst, at, sems):
+    lanes = pl.ds(at.start, IMG_CHUNK)
+    c = pltpu.make_async_copy(src.at[:, lanes], dst.at[:, lanes], sems.at[at.start // IMG_CHUNK])
+    c.start()
+    return c
+
+
 def first_kernel(
     txt_hbm, txt_raw_hbm, img_hbm, img_raw_hbm, w0, w1, w2, w3, er_ref, col_ref, label_ref,
-    img_emb_hbm, img_own_hbm, wt_hbm, inv_ref, img_part_ref, along_ref, txt_part_ref,
+    img_emb_hbm, img_own_hbm, wt_hbm, inv_ref, img_part_hbm, along_ref, txt_part_ref,
     txt_s, txt_raw, img_s, img_raw, wi_s, wt_s, txt_emb, txt_own_t, img_emb_t, img_own_t, ec_s, g_s,
-    sems, out_sems,
+    img_part_s, sems, out_sems, strip_sems,
 ):
     pairs = txt_s.shape[0]
     block = pairs // 4
@@ -216,8 +226,9 @@
         c.start()
 
     def finish(at, img_part, along):
-        img_part_ref[:, at] = img_part
+        img_part_s[:, at] = img_part
         along_ref[:, at] = along
+        saves.append(save_strip(img_part_s, img_part_hbm, at, strip_sems))
 
     score_tile(txt_emb, txt_own_t, img_emb_t, er_ref, ec_s, label_ref, g_s, finish)
     text_part(g_s, img_emb_t, cols, txt_part_ref)
@@ -244,28 +255,33 @@
 
 def second_kernel(
     feats, wt, img_emb_hbm, er_ref, img_part_hbm, along_in,
-    img_part_ref, along_ref, txt_part_ref,
-    img_emb_t, img_part_s, txt_emb, txt_own_t, lse_s, ec_s, g_s, sems,
+    img_part_out, along_ref, g_hbm,
+    img_emb_t, img_part_s, txt_emb, txt_own_t, lse_s, ec_s, g_s, sems, part_sems, g_sems,
 ):
     loads = copies([(img_emb_hbm, img_emb_t), (img_part_hbm, img_part_s)], sems)
     stand_half(feats, lax.axis_index("core"), lse_s, ec_s)
     project_texts(feats, wt, txt_emb, txt_own_t)
     loads[0].wait()
 
+    saves = []
+
     def finish(at, img_part, along):
         if at.start == 0:
             loads[1].wait()
-        img_part_ref[:, at] = img_part_s[:, at] + img_part
+        img_part_s[:, at] = img_part_s[:, at] + img_part
         along_ref[:, at] = along_in[:, at] + along
+        saves.append(save_strip(img_part_s, img_part_out, at, part_sems))
+        saves.append(save_strip(g_s, g_hbm, at, g_sems))
 
     score_tile(txt_emb, txt_own_t, img_emb_t, er_ref, ec_s, None, g_s, finish)
-    text_part(g_s, img_emb_t, txt_own_t.shape[0], txt_part_ref)
+    for c in saves:
+        c.wait()
 
 
 def last_kernel(
     feats, wt, img_emb_hbm, er_ref, img_part_hbm, along_in, img_own_hbm, inv_ref, img_hbm,
-    pieces_ref, txt_part_ref,
-    img_emb_t, img_part_s, img_own_t, img_s, txt_emb, txt_own_t, lse_s, ec_s, g_s, d_raw, sems,
+    pieces_ref, g_hbm,
+    img_emb_t, img_part_s, img_own_t, img_s, txt_emb, txt_own_t, lse_s, ec_s, g_s, d_raw, sems, g_sems,
 ):
     loads = copies(
         [
@@ -277,6 +293,8 @@
     stand_half(feats, 1 - lax.axis_index("core"), lse_s, ec_s)
     project_texts(feats, wt, txt_emb, txt_own_t)
     loads[0].wait()
+
+    saves = []
 
     def finish(at, img_part, along):
         if at.start == 0:
@@ -287,6 +305,7 @@
         d_raw[:, at] = (
             (grad - img_own_t[:, at] * toward) * (scale_logit * inv_ref[:, at])
         ).astype(BF)
+        saves.append(save_strip(g_s, g_hbm, at, g_sems))
 
     score_tile(txt_emb, txt_own_t, img_emb_t, er_ref, ec_s, None, g_s, finish)
     loads[3].wait()
@@ -299,15 +318,30 @@
                 pieces_ref[r * across + k // cb + c] = part[
                     r * rb : (r + 1) * rb, c * cb : (c + 1) * cb
                 ].astype(BF)
-    text_part(g_s, img_emb_t, txt_own_t.shape[0], txt_part_ref)
-
-
-def text_total_kernel(part_a, part_b, carry, out_ref):
-    half = part_a.shape[1]
+    for c in saves:
+        c.wait()
+
+
+def text_total_kernel(g_a, g_b, img_emb_hbm, carry, out_ref, own_s, g_s, own_sem, sems):
+    half = g_a.shape[0]
+    block = half // 4
     core = lax.axis_index("core")
-    for place, part in ((core, part_a), (1 - core, part_b)):
-        at = pl.ds(pl.multiple_of(place * half, half), half)
-        out_ref[:, at] = part[...] + carry[:, at].astype(F32)
+    own = pltpu.make_async_copy(img_emb_hbm.at[pl.ds(0, own_s.shape[0]), :], own_s, own_sem)
+    own.start()
+    moves = [
+        (g.at[pl.ds(r, block), :], g_s.at[pl.ds(n * half + r, block), :])
+        for n, g in enumerate((g_a, g_b))
+        for r in range(0, half, block)
+    ]
+    loads = copies(moves, sems)
+    own.wait()
+    for n, place in enumerate((core, 1 - core)):
+        for m in range(4):
+            loads[4 * n + m].wait()
+            r = n * half + m * block
+            part = scale_logit * dot(own_s[...], g_s[r : r + block, :], NT)
+            at = pl.ds(pl.multiple_of(place * half + m * block, block), block)
+            out_ref[:, at] = part + carry[:, at].astype(F32)
 
 
 def local(sizes, img_feats, txt_feats, img_weight, txt_weight, row_lse, col_lse, labels):
@@ -350,7 +384,7 @@
             (shape((half + lse.shape[0], txt_in), BF), VMEM),
             (shape((cols, img_in + txt_in), BF), VMEM),
         ],
-        [pltpu.SemaphoreType.DMA((3,))],
+        [pltpu.SemaphoreType.DMA((10,))],
         0,
         0,
     )(txt_feats, lse, img_weight.T, txt_weight.T)
@@ -390,7 +424,7 @@
             (shape((cols, pairs), F32), ANY),
             (shape((width, txt_in), BF), ANY),
             (shape((1, pairs), F32), VMEM),
-            (shape((cols, pairs), F32), VMEM),
+            (shape((cols, pairs), F32), ANY),
             (shape((1, pairs), F32), VMEM),
             (shape((cols, pairs), BF), VMEM),
         ],
@@ -407,8 +441,10 @@
             pltpu.VMEM((cols, pairs), F32),
             pltpu.VMEM((pairs, 128), F32),
             pltpu.VMEM((pairs, pairs), BF),
+            pltpu.VMEM((cols, pairs), F32),
             pltpu.SemaphoreType.DMA((16,)),
             pltpu.SemaphoreType.DMA((3,)),
+            pltpu.SemaphoreType.DMA((pairs // IMG_CHUNK,)),
         ],
         tile_flops,
         4 * pairs * width * 2,
@@ -420,6 +456,7 @@
     feats_a, along = lax.optimization_barrier((feats_a, along))
     feats_b = send(feats_a, swap)
 
+    strip_sems = [pltpu.SemaphoreType.DMA((pairs // IMG_CHUNK,))]
     half_scratch = [
         pltpu.VMEM((half, width), BF),
         pltpu.VMEM((cols, half), BF),
@@ -427,25 +464,25 @@
         pltpu.VMEM((half, 128), F32),
         pltpu.VMEM((half, pairs), BF),
     ]
-    img_part, along, txt_a = call(
+    img_part, along, g_a = call(
         second_kernel,
         [VMEM, VMEM, ANY, VMEM, ANY, VMEM],
         [
-            (shape((cols, pairs), F32), VMEM),
+            (shape((cols, pairs), F32), ANY),
             (shape((1, pairs), F32), VMEM),
-            (shape((cols, half), F32), VMEM),
+            (shape((half, pairs), BF), ANY),
         ],
         [pltpu.VMEM((width, pairs), BF), pltpu.VMEM((cols, pairs), F32)]
         + half_scratch
-        + [pltpu.SemaphoreType.DMA((2,))],
+        + [pltpu.SemaphoreType.DMA((2,))] + strip_sems * 2,
         tile_flops // 2,
         2 * pairs * width * 2,
         pairs * half,
     )(feats_a, wt, img_emb_t, er, img_part, along)
-    pieces, txt_b = call(
+    pieces, g_b = call(
         last_kernel,
         [VMEM, VMEM, ANY, VMEM, ANY, VMEM, ANY, VMEM, ANY],
-        [(shape((n_dp, cols * img_in // (128 * n_dp), 128), BF), VMEM), (shape((cols, half), F32), VMEM)],
+        [(shape((n_dp, cols * img_in // (128 * n_dp), 128), BF), VMEM), (shape((half, pairs), BF), ANY)],
         [
             pltpu.VMEM((width, pairs), BF),
             pltpu.VMEM((cols, pairs), F32),
@@ -453,7 +490,7 @@
             pltpu.VMEM((pairs, img_in), BF),
         ]
         + half_scratch
-        + [pltpu.VMEM((cols, pairs), BF), pltpu.SemaphoreType.DMA((4,))],
+        + [pltpu.VMEM((cols, pairs), BF), pltpu.SemaphoreType.DMA((4,))] + strip_sems,
         tile_flops // 2,
         2 * pairs * width * 2,
         pairs * half,
@@ -466,12 +503,17 @@
     back = lax.all_to_all(spread, DP, 0, 0, tiled=True)
     (txt_total,) = call(
         text_total_kernel,
-        [VMEM] * 3,
+        [ANY, ANY, ANY, VMEM],
         [(shape((cols, pairs), F32), VMEM)],
-        [],
+        [
+            pltpu.VMEM((cols, pairs), BF),
+            pltpu.VMEM((pairs, pairs), BF),
+            pltpu.SemaphoreType.DMA,
+            pltpu.SemaphoreType.DMA((8,)),
+        ],
         0,
         10 * cols * pairs,
-    )(txt_a, txt_b, txt_carry)
+    )(g_a, g_b, img_emb_t, txt_carry)
     across_pieces = img_in // 128
     tiles = back.reshape(n_dp // across_pieces, across_pieces, pieces.shape[1], 128)
     weight_total = tiles.transpose(0, 2, 1, 3).reshape(cols, img_in).astype(F32)

time: 144 us -> 141 us (0.979)
  waiting for transfers between devices: 18.7 us -> 10.1 us
  Pallas kernels: 77.6 us -> 83.6 us
    all_to_all x1, waiting for transfers between devices: 12.5 us -> 3.94 us  [local(): back = lax.all_to_all(spread, DP, 0, 0, tiled=True)]
    pallas_call x1, Pallas kernels: 2.88 us -> 11.5 us  [local(): call(text_total_kernel, [ANY, ANY, ANY, VMEM], [(shape((cols, pairs), F32...]
  transfers between devices with their start and end apart: 10 -> 10, of which waited for: 4 -> 4; matrix products, arithmetic and copies ran while one was open for 1% -> 1% of each run, Pallas kernels for 51% -> 56%
where the time goes in v2:
time: 141 us; the launch traced here: 142 us
  Pallas kernels  83.6 us (59%)
  blocking collectives  27.5 us (20%)
  starting transfers between devices  13.1 us (9%)
  waiting for transfers between devices  10.1 us (7%)
  local copies, waits for them, and re-layouts  4.96 us (4%)
  other arithmetic  1.46 us (1%)
    pallas_call x1, Pallas kernels, local(): call(first_kernel, [ANY] * 4 + [VMEM] * 7, [(shape((width, pairs), BF), A...  36.7 us
    all_to_all x1, blocking collectives, local(): got = lax.all_to_all(pieces, DP, 0, 0, tiled=True)  27.5 us
    pallas_call x1, Pallas kernels, local(): call(text_total_kernel, [ANY, ANY, ANY, VMEM], [(shape((cols, pairs), F32...  11.5 us
    pallas_call x1, Pallas kernels, local(): call(last_kernel, [VMEM, VMEM, ANY, VMEM, ANY, VMEM, ANY, VMEM, ANY], [(s...  11.4 us
    pallas_call x1, Pallas kernels, local(): call(second_kernel, [VMEM, VMEM, ANY, VMEM, ANY, VMEM], [(shape((cols, pa...  10.9 us
    pallas_call x1, Pallas kernels, local(): call(near_kernel, [ANY, ANY, VMEM, VMEM, VMEM], [(shape((2 * cols, pairs)...  9.4 us
    ppermute x9, starting transfers between devices, send(): return lax.ppermute(a, AXES, route)  8.2 us
    ppermute x9, waiting for transfers between devices, send(): return lax.ppermute(a, AXES, route)  6.21 us
  transfers between devices with their start and end apart: 10, of which 4 were waited for; matrix products, arithmetic and copies ran while one was open for 1% of the time, Pallas kernels for 56%

profile of v2, /device:TPU:24, one launch (start us, length us, event | category | flops | bytes accessed | tf_op | source)
XLA Modules:
  0.0 141.8 jit_solution(11901011578644302785)
XLA Ops:
  0.6 3.7 %shard_map.86 = (bf16[1040,768]{1,0:T(8,128)(2,1)}, bf16[192,1792]{1,0:T(8,128)(2,1)}) custom-call(bf16[2048,768]{1,0:T(8,128)(2,1)} %txt_hbm.5, f32[16,128]{1,0:T(8,128)} %bitcast.23, bf16[192,1024]{1,0:T(8,128)(2,1)} %bitcast.21, bf16[192,768]{1,0:T(8,128)(2,1)} %bitcast.22), custom_call_target="tpu_custom_call" | custom-call | tf_op jit(solution)/shard_map/pallas_call | solution.py:380
  4.3 2.0 %collective-permute-start = (bf16[1040,768]{1,0:T(8,128)(2,1)}, bf16[1040,768]{1,0:T(8,128)(2,1)S(1)}, u32[]{:S(2)}, u32[]{:S(2)}) collective-permute-start(bf16[1040,768]{1,0:T(8,128)(2,1)} %get-tuple-element.23), channel_id=1, source_target_pairs={{0,4},{1,5},{2,6},{3,7},{4,8},{5,9},{6,10},{7,11},{8,12},{9,13},{1... | collective-permute-start | bytes 4792328 | tf_op jit(solution)/shard_map/ppermute | solution.py:370
  6.3 0.0 collective-permute-start.1
  6.3 0.2 collective-permute-start.2
  6.6 2.1 %collective-permute-done.1.w1 = bf16[192,1792]{1,0:T(8,128)(2,1)S(1)} collective-permute-done((bf16[192,1792]{1,0:T(8,128)(2,1)}, bf16[192,1792]{1,0:T(8,128)(2,1)S(1)}, u32[]{:S(2)}, u32[]{:S(2)}) %collective-permute-start.1) | collective-permute-done | bytes 688160 | tf_op jit(solution)/shard_map/ppermute | solution.py:370
  8.7 0.0 copy-start
  8.7 0.8 copy-done
  9.5 9.4 %shard_map.87 = (f32[384,2048]{1,0:T(8,128)}, f32[2048,384]{1,0:T(8,128)}, f32[1,512]{1,0:T(1,128)}) custom-call(bf16[2048,1024]{1,0:T(8,128)(2,1)} %img_hbm.5, bf16[2048,768]{1,0:T(8,128)(2,1)} %txt_hbm.5, bf16[192,1792]{1,0:T(8,128)(2,1)} %get-tuple-element.24.w0, bf16[192,1792]{1,0:T(8,128)(2,1)} %copy-done, f32[1,512]{1,0:T(1,128)} %bitcast.25), custom_call_target="tpu_custom_call" | custom-call | tf_op jit(solution)/shard_map/pallas_call | solution.py:395
  18.9 0.2 collective-permute-start.4
  19.2 1.3 collective-permute-start.5
  20.4 2.0 %collective-permute-start.6 = (f32[1,512]{1,0:T(1,128)}, f32[1,512]{1,0:T(1,128)S(1)}, u32[]{:S(2)}, u32[]{:S(2)}) collective-permute-start(f32[1,512]{1,0:T(1,128)} %get-tuple-element.27), channel_id=1, source_target_pairs={{0,3},{1,2},{2,1},{3,0},{4,7},{5,6},{6,5},{7,4},{8,11},{9,10},{10,... | collective-permute-start | bytes 6152 | tf_op jit(solution)/shard_map/ppermute | solution.py:370
  22.4 3.3 %collective-permute-done.2.w2 = bf16[192,1792]{1,0:T(8,128)(2,1)S(1)} collective-permute-done((bf16[192,1792]{1,0:T(8,128)(2,1)}, bf16[192,1792]{1,0:T(8,128)(2,1)S(1)}, u32[]{:S(2)}, u32[]{:S(2)}) %collective-permute-start.2) | collective-permute-done | bytes 688160 | tf_op jit(solution)/shard_map/ppermute | solution.py:370
  25.7 0.0 copy-start.4
  25.7 0.4 collective-permute-start.3
  26.1 0.0 collective-permute-done.4
  26.1 0.7 broadcast_select_fusion.5
  26.8 0.0 collective-permute-done.5
  26.8 0.0 collective-permute-done.6
  26.8 0.6 pad_maximum_fusion.er_ref
  27.4 0.8 collective-permute-done.3.w3
  28.2 0.0 copy-start.5
  28.2 0.0 copy-done.4
  28.2 0.9 copy-done.5
  29.1 36.7 %shard_map.88 = (bf16[768,2048]{1,0:T(8,128)(2,1)}, f32[192,2048]{1,0:T(8,128)}, bf16[768,768]{1,0:T(8,128)(2,1)}, f32[1,2048]{1,0:T(1,128)}, f32[192,2048]{1,0:...) custom-call(bf16[2048,768]{1,0:T(8,128)(2,1)} %txt_hbm.5, f32[2048,384]{1,0:T(8,128)} %get-tuple-element.25.txt_raw_hbm, ...), custom_call_target="tpu_custom_call" | custom-call | tf_op jit(solution)/shard_map/pallas_call | solution.py:419
  65.8 0.0 collective-permute-done.feats
  65.8 0.0 copy-start.2
  65.8 0.2 collective-permute-start.7
  66.0 1.9 %collective-permute-start.8 = (bf16[192,2048]{1,0:T(8,128)(2,1)}, bf16[192,2048]{1,0:T(8,128)(2,1)S(1)}, u32[]{:S(2)}, u32[]{:S(2)}) collective-permute-start(bf16[192,2048]{1,0:T(8,128)(2,1)} %get-tuple-element.39), channel_id=1, source_target_pairs={{0,4},{1,5},{2,6},{3,7},{4,8},{5,9},{6,10},{7,11},{8,12},{9,13},{1... | collective-permute-start | bytes 2359304 | tf_op jit(solution)/shard_map/ppermute | solution.py:370
  67.9 0.0 copy-done.2
  67.9 10.9 %shard_map.89 = (f32[192,2048]{1,0:T(8,128)}, f32[1,2048]{1,0:T(1,128)}, bf16[1024,2048]{1,0:T(8,128)(2,1)}) custom-call(bf16[1040,768]{1,0:T(8,128)(2,1)} %copy-done.2, bf16[768,768]{1,0:T(8,128)(2,1)} %get-tuple-element.30.wt, bf16[768,2048]{1,0:T(8,128)(2,1)} %get-tuple-element.31.img_emb_hbm, f32[1,2048]{1,0:T(1,128)} %pad_maximum_fusion.er_ref, ...), custom_call_target="tpu_custom_call" | custom-call | tf_op jit(solution)/shard_map/pallas_call | solution.py:467
  78.8 0.0 collective-permute-done.7.feats
  78.8 0.0 copy-start.1
  78.8 1.3 copy-done.1
  80.1 11.4 %shard_map.90 = (bf16[64,24,128]{2,1,0:T(8,128)(2,1)}, bf16[1024,2048]{1,0:T(8,128)(2,1)}) custom-call(bf16[1040,768]{1,0:T(8,128)(2,1)} %copy-done.1, bf16[768,768]{1,0:T(8,128)(2,1)} %get-tuple-element.30.wt, bf16[768,2048]{1,0:T(8,128)(2,1)} %get-tuple-element.31.img_emb_hbm, f32[1,2048]{1,0:T(1,128)} %pad_maximum_fusion.er_ref, ...), custom_call_target="tpu_custom_call" | custom-call | tf_op jit(solution)/shard_map/pallas_call | solution.py:482
  91.5 0.0 collective-permute-done.8.carry
  91.6 0.0 copy-start.3
  91.6 27.5 %all_to_all.10 = bf16[64,24,128]{2,1,0:T(8,128)(2,1)S(1)} all-to-all(bf16[64,24,128]{2,1,0:T(8,128)(2,1)} %get-tuple-element.40), channel_id=1, replica_groups=mesh['yl'=2,'x'=4,'z'=8,'yh'=2,'core'=2] {'yl','x','z'}, dimensions={0} | all-to-all | bytes 786432 | tf_op jit(solution)/shard_map/all_to_all | solution.py:500
  119.1 0.1 reduce_sum.12
  119.2 0.8 broadcast_in_dim.10
  120.0 4.9 %all-to-all-start.1 = ((bf16[64,24,128]{2,1,0:T(8,128)(2,1)}), bf16[64,24,128]{2,1,0:T(8,128)(2,1)S(1)}, u32[]{:S(2)}, u32[]{:S(2)}) async-start(bf16[64,24,128]{2,1,0:T(8,128)(2,1)} %broadcast_in_dim.10), calls=%async_computation.1 | async-start | bytes 786432 | tf_op jit(solution)/shard_map/all_to_all | solution.py:503
  124.9 0.0 copy-done.3
  124.9 11.5 %shard_map.91 = f32[192,2048]{1,0:T(8,128)} custom-call(bf16[1024,2048]{1,0:T(8,128)(2,1)} %get-tuple-element.41.g_a, bf16[1024,2048]{1,0:T(8,128)(2,1)} %get-tuple-element.42.g_b, bf16[768,2048]{1,0:T(8,128)(2,1)} %get-tuple-element.31.img_emb_hbm, bf16[192,2048]{1,0:T(8,128)(2,1)} %copy-done.3), custom_call_target="tpu_custom_call" | custom-call | tf_op jit(solution)/shard_map/pallas_call | solution.py:504
  136.4 3.9 %all-to-all-done.1 = bf16[64,24,128]{2,1,0:T(8,128)(2,1)S(1)} async-done(((bf16[64,24,128]{2,1,0:T(8,128)(2,1)}), bf16[64,24,128]{2,1,0:T(8,128)(2,1)S(1)}, u32[]{:S(2)}, u32[]{:S(2)}) %all-to-all-start.1) | async-done | bytes 393248 | tf_op jit(solution)/shard_map/all_to_all | solution.py:503
  140.3 0.1 convert_bitcast_fusion
  140.4 0.1 copy.9
  140.5 1.0 copy.12
  (2 shorter events, 0.0 us)
Async XLA Ops:
  4.3 61.4 %collective-permute-start = (bf16[1040,768]{1,0:T(8,128)(2,1)}, bf16[1040,768]{1,0:T(8,128)(2,1)S(1)}, u32[]{:S(2)}, u32[]{:S(2)}) collective-permute-start(bf16[1040,768]{1,0:T(8,128)(2,1)} %get-tuple-element.23), channel_id=1, source_target_pairs={{0,4},{1,5},{2,6},{3,7},{4,8},{5,9},{6,10},{7,11},{8,12},{9,13},{1... | collective-permute-start | bytes 4792328 | tf_op jit(solution)/shard_map/ppermute | solution.py:370
  6.3 2.4 %collective-permute-start.1 = (bf16[192,1792]{1,0:T(8,128)(2,1)}, bf16[192,1792]{1,0:T(8,128)(2,1)S(1)}, u32[]{:S(2)}, u32[]{:S(2)}) collective-permute-start(bf16[192,1792]{1,0:T(8,128)(2,1)} %get-tuple-element.24.w0), channel_id=1, source_target_pairs={{0,1},{1,0},{2,3},{3,2},{4,5},{5,4},{6,7},{7,6},{8,9},{9,8},{10,11... | collective-permute-start | bytes 2064392 | tf_op jit(solution)/shard_map/ppermute | solution.py:370
  6.3 19.4 %collective-permute-start.2 = (bf16[192,1792]{1,0:T(8,128)(2,1)}, bf16[192,1792]{1,0:T(8,128)(2,1)S(1)}, u32[]{:S(2)}, u32[]{:S(2)}) collective-permute-start(bf16[192,1792]{1,0:T(8,128)(2,1)} %get-tuple-element.24.w0), channel_id=1, source_target_pairs={{0,130},{1,131},{2,128},{3,129},{4,134},{5,135},{6,132},{7,133},{8... | collective-permute-start | bytes 2064392 | tf_op jit(solution)/shard_map/ppermute | solution.py:370
  8.7 0.8 copy-start
  18.9 7.1 %collective-permute-start.4 = (f32[1,512]{1,0:T(1,128)}, f32[1,512]{1,0:T(1,128)S(1)}, u32[]{:S(2)}, u32[]{:S(2)}) collective-permute-start(f32[1,512]{1,0:T(1,128)} %get-tuple-element.27), channel_id=1, source_target_pairs={{0,1},{1,0},{2,3},{3,2},{4,5},{5,4},{6,7},{7,6},{8,9},{9,8},{10,11... | collective-permute-start | bytes 6152 | tf_op jit(solution)/shard_map/ppermute | solution.py:370
  19.2 7.6 %collective-permute-start.5 = (f32[1,512]{1,0:T(1,128)}, f32[1,512]{1,0:T(1,128)S(1)}, u32[]{:S(2)}, u32[]{:S(2)}) collective-permute-start(f32[1,512]{1,0:T(1,128)} %get-tuple-element.27), channel_id=1, source_target_pairs={{0,2},{1,3},{2,0},{3,1},{4,6},{5,7},{6,4},{7,5},{8,10},{9,11},{10,... | collective-permute-start | bytes 6152 | tf_op jit(solution)/shard_map/ppermute | solution.py:370
  20.4 6.4 %collective-permute-start.6 = (f32[1,512]{1,0:T(1,128)}, f32[1,512]{1,0:T(1,128)S(1)}, u32[]{:S(2)}, u32[]{:S(2)}) collective-permute-start(f32[1,512]{1,0:T(1,128)} %get-tuple-element.27), channel_id=1, source_target_pairs={{0,3},{1,2},{2,1},{3,0},{4,7},{5,6},{6,5},{7,4},{8,11},{9,10},{10,... | collective-permute-start | bytes 6152 | tf_op jit(solution)/shard_map/ppermute | solution.py:370
  25.7 2.5 %copy-start.4 = (bf16[192,1792]{1,0:T(8,128)(2,1)}, bf16[192,1792]{1,0:T(8,128)(2,1)S(1)}, u32[]{:S(2)}) copy-start(bf16[192,1792]{1,0:T(8,128)(2,1)S(1)} %collective-permute-done.2.w2) | copy-start | bytes 2064388
  25.7 2.5 %collective-permute-start.3 = (bf16[192,1792]{1,0:T(8,128)(2,1)S(1)}, bf16[192,1792]{1,0:T(8,128)(2,1)S(1)}, u32[]{:S(2)}, u32[]{:S(2)}) collective-permute-start(bf16[192,1792]{1,0:T(8,128)(2,1)S(1)} %collective-permute-done.2.w2), channel_id=1, source_target_pairs={{0,1},{1,0},{2,3},{3,2},{4,5},{5,4},{6,7},{7,6},{8,9},{9,8},{10,11... | collective-permute-start | bytes 2064392 | tf_op jit(solution)/shard_map/ppermute | solution.py:370
  28.2 0.9 copy-start.5
  65.8 2.2 %copy-start.2 = (bf16[1040,768]{1,0:T(8,128)(2,1)}, bf16[1040,768]{1,0:T(8,128)(2,1)S(1)}, u32[]{:S(2)}) copy-start(bf16[1040,768]{1,0:T(8,128)(2,1)S(1)} %collective-permute-done.feats) | copy-start | bytes 4792324
  65.8 13.0 %collective-permute-start.7 = (bf16[1040,768]{1,0:T(8,128)(2,1)S(1)}, bf16[1040,768]{1,0:T(8,128)(2,1)S(1)}, u32[]{:S(2)}, u32[]{:S(2)}) collective-permute-start(bf16[1040,768]{1,0:T(8,128)(2,1)S(1)} %collective-permute-done.feats), channel_id=1, source_target_pairs={{0,1},{1,0},{2,3},{3,2},{4,5},{5,4},{6,7},{7,6},{8,9},{9,8},{10,11... | collective-permute-start | bytes 4792328 | tf_op jit(solution)/shard_map/ppermute | solution.py:370
  66.0 25.6 %collective-permute-start.8 = (bf16[192,2048]{1,0:T(8,128)(2,1)}, bf16[192,2048]{1,0:T(8,128)(2,1)S(1)}, u32[]{:S(2)}, u32[]{:S(2)}) collective-permute-start(bf16[192,2048]{1,0:T(8,128)(2,1)} %get-tuple-element.39), channel_id=1, source_target_pairs={{0,4},{1,5},{2,6},{3,7},{4,8},{5,9},{6,10},{7,11},{8,12},{9,13},{1... | collective-permute-start | bytes 2359304 | tf_op jit(solution)/shard_map/ppermute | solution.py:370
  78.8 1.3 copy-start.1
  91.6 33.3 %copy-start.3 = (bf16[192,2048]{1,0:T(8,128)(2,1)}, bf16[192,2048]{1,0:T(8,128)(2,1)S(1)}, u32[]{:S(2)}) copy-start(bf16[192,2048]{1,0:T(8,128)(2,1)S(1)} %collective-permute-done.8.carry) | copy-start | bytes 2359300
  120.0 20.3 %all-to-all-start.1 = ((bf16[64,24,128]{2,1,0:T(8,128)(2,1)}), bf16[64,24,128]{2,1,0:T(8,128)(2,1)S(1)}, u32[]{:S(2)}, u32[]{:S(2)}) async-start(bf16[64,24,128]{2,1,0:T(8,128)(2,1)} %broadcast_in_dim.10), calls=%async_computation.1 | async-start | bytes 786432 | tf_op jit(solution)/shard_map/all_to_all | solution.py:503
